TPU v7x, 32 devices: a whole 2x2x4 slice. The times are simulated.
32 devices in a mesh: ctx: 8 (over y, x, core), exp: 4 (over z).
Axes of the slice: x: 2, y: 2, z: 4, core: 2. Of those that a mesh axis runs over, the one named last changes fastest.
Arguments:
- mixer_x: bfloat16 [1024, 4096], P('ctx', 'exp')
- mixer_z: bfloat16 [1024, 4096], P('ctx', 'exp'), may hold values from -6 to 6
- step_raw: float32 [1024, 4096], P('ctx', 'exp')
- input_b: float32 [16, 1024], P(None, 'ctx'), may hold values from -6 to 6
- output_c: float32 [16, 1024], P(None, 'ctx'), may hold values from -4 to 4
- decay_log: float32 [16, 4096], P(None, 'exp')
- skip_gain: float32 [4096], P('exp'), may hold values from 0.5 to 1.5
- out_proj: bfloat16 [4096, 2048], P('exp'), may hold values from -0.09375 to 0.09375
- residual: bfloat16 [1024, 2048], P(('ctx', 'exp')), may hold values from -6 to 6
- norm_gain: float32 [2048], replicated, may hold values from 0.1 to 1.9
- gate_proj: bfloat16 [4, 2048, 8192], P('exp', None, 'ctx'), may hold values from -0.125 to 0.125
- up_proj: bfloat16 [4, 2048, 8192], P('exp', None, 'ctx'), may hold values from -0.125 to 0.125
- down_proj: bfloat16 [4, 8192, 2048], P('exp', 'ctx'), may hold values from -0.0625 to 0.0625
- expert_ids: int32 [1024, 2], P(('ctx', 'exp')), may hold values from 0 to 3, as said below
- slot_ids: int32 [1024, 2], P(('ctx', 'exp')), may hold values from -1 to 15, as said below
- route_weight: float32 [1024, 2], P(('ctx', 'exp')), may hold values from 0.2 to 1
Outputs:
- layer_out: bfloat16 [1024, 2048], P(('ctx', 'exp'))
Inputs may be any that keep to these rules, and one draw needn't show every extreme that they name: `expert_ids`: A token's two ids differ. In every draw one expert is named by at least 16 tokens of every device's 32 tokens. `slot_ids`: A copy's slot is its rank among the copies of the same device's tokens to the same expert, taken in order of token and then of choice, or -1 where that rank is 16 or more.
All inputs are finite; a program needn't handle non-finite values.
Results may differ from a plain program's by a relative error of at most 0.017.
Values may be sent and summed in bfloat16 or wider, within the bound.
A program may use at most 64 MiB of HBM per device.

v0:
```python
import jax
import jax.numpy as jnp
from jax import lax
from jax.sharding import PartitionSpec as P

EPSILON = 1e-05


def prefix(array, axis, combine, identity):
    count, here = (lax.axis_size(axis), lax.axis_index(axis))
    everything = jax.tree.map(
        lambda part, kind: lax.all_gather(part.astype(kind), axis),
        array,
        (jnp.bfloat16, jnp.bfloat16),
    )
    start = jax.tree.map(
        lambda part, zero: jnp.broadcast_to(jnp.asarray(zero, part.dtype), part.shape),
        array,
        identity,
    )

    def lap(k, before):
        reached = k < here
        new = combine(
            before, jax.tree.map(lambda part, own: part[k].astype(own.dtype), everything, array)
        )
        return jax.tree.map(lambda a, b: jnp.where(reached, a, b), new, before)

    return lax.fori_loop(0, count, lap, start)


def link_states(earlier, later):
    return (earlier[0] * later[0], later[0] * earlier[1] + later[1])


def local_recurrence(step_size, x_float, input_b, output_c, decay_rate):
    tokens = step_size.shape[0]
    width = step_size.shape[1]
    states = decay_rate.shape[0]
    sub_len = tokens // 16
    step_blocks = step_size.reshape(16, sub_len, width)
    x_blocks = x_float.reshape(16, sub_len, width)
    b_blocks = input_b.T.reshape(16, sub_len, states)
    c_blocks = output_c.T.reshape(16, sub_len, states)

    def advance(carry, blocks):
        state, run_step = carry
        step_blk, x_blk, b_blk, c_blk = blocks
        outputs = []
        totals = []
        for inner_pos in range(sub_len):
            step_now = step_blk[inner_pos]
            state = (
                jnp.exp(step_now[None, :] * decay_rate) * state
                + (step_now * x_blk[inner_pos])[None, :] * b_blk[inner_pos][:, None]
            )
            run_step = run_step + step_now
            outputs.append(jnp.sum(c_blk[inner_pos][:, None] * state, axis=0))
            totals.append(run_step)
        return ((state, run_step), (jnp.stack(outputs), jnp.stack(totals)))

    start = (jnp.zeros((states, width), jnp.float32), jnp.zeros((width,), jnp.float32))
    finals, outs = lax.scan(advance, start, (step_blocks, x_blocks, b_blocks, c_blocks))
    local_y = outs[0].reshape(tokens, width)
    cumulative = outs[1].reshape(tokens, width)
    return (finals[0], finals[1], local_y, cumulative)


def on_device(
    mixer_x,
    mixer_z,
    step_raw,
    input_b,
    output_c,
    decay_log,
    skip_gain,
    out_proj,
    residual,
    norm_gain,
    gate_proj,
    up_proj,
    down_proj,
    expert_ids,
    slot_ids,
    route_weight,
):
    n_exp = lax.axis_size("exp")
    step_size = jax.nn.softplus(step_raw)
    decay_rate = -jnp.exp(decay_log)
    x_float = mixer_x.astype(jnp.float32)
    final_state, total_step, local_y, cumulative = local_recurrence(
        step_size, x_float, input_b, output_c, decay_rate
    )
    through_final = jnp.exp(total_step[None, :] * decay_rate)
    identity = (jnp.ones_like(through_final), jnp.zeros_like(final_state))
    carried = prefix((through_final, final_state), "ctx", link_states, identity)
    carried_state = carried[1]
    correction = jnp.zeros_like(local_y)
    for state_index in range(decay_rate.shape[0]):
        weight_row = (
            jnp.exp(cumulative * decay_rate[state_index][None, :])
            * carried_state[state_index][None, :]
        )
        correction = correction + output_c[state_index][:, None] * weight_row
    mixer_y = local_y + correction + skip_gain * x_float
    gated = (mixer_y * jax.nn.silu(mixer_z.astype(jnp.float32))).astype(jnp.bfloat16)
    partial_out = jnp.dot(gated, out_proj, preferred_element_type=jnp.float32)
    tok_dev = residual.shape[0]
    model_width = residual.shape[1]
    summed = lax.psum(partial_out.astype(jnp.bfloat16), "exp").astype(jnp.float32)
    mixer_out = lax.dynamic_slice_in_dim(summed, lax.axis_index("exp") * tok_dev, tok_dev, 0)
    hidden_one = (residual.astype(jnp.float32) + mixer_out).astype(jnp.bfloat16)
    hidden_one = lax.optimization_barrier(hidden_one)
    hidden_float = hidden_one.astype(jnp.float32)
    inv_rms = lax.rsqrt(jnp.mean(hidden_float * hidden_float, axis=-1, keepdims=True) + EPSILON)
    normed = (hidden_float * inv_rms * norm_gain).astype(jnp.bfloat16)
    experts_local = gate_proj.shape[0]
    experts_all = experts_local * n_exp
    capacity = max(2, expert_ids.shape[1] * tok_dev // experts_all)
    slot_count = experts_all * capacity
    per_device = experts_local * capacity
    target_index = jnp.where(slot_ids >= 0, expert_ids * capacity + slot_ids, -1)
    slot_iota = jnp.arange(slot_count, dtype=jnp.int32)
    select = jnp.any(target_index[None, :, :] == slot_iota[:, None, None], axis=-1).astype(
        jnp.bfloat16
    )
    dispatch = jnp.dot(select, normed, preferred_element_type=jnp.float32).astype(jnp.bfloat16)
    arrived = lax.all_to_all(
        dispatch.reshape(n_exp, per_device, model_width),
        "exp",
        split_axis=0,
        concat_axis=0,
        tiled=True,
    )
    piece = lax.all_gather(arrived, "ctx", axis=0, tiled=True)
    outputs = []
    local_index = 0
    rows_here = piece.reshape(-1, piece.shape[2])
    gate_value = jnp.dot(rows_here, gate_proj[local_index], preferred_element_type=jnp.float32)
    up_value = jnp.dot(rows_here, up_proj[local_index], preferred_element_type=jnp.float32)
    hidden = (jax.nn.silu(gate_value) * up_value).astype(jnp.bfloat16)
    outputs.append(hidden.reshape(piece.shape[0], capacity, hidden.shape[1]))
    hidden_rows = outputs[0]
    outputs = []
    local_index = 0
    rows_here = hidden_rows.reshape(-1, hidden_rows.shape[2])
    product = jnp.dot(rows_here, down_proj[local_index], preferred_element_type=jnp.float32)
    outputs.append(product.reshape(n_exp * lax.axis_size("ctx"), capacity, model_width))
    expert_out = lax.psum_scatter(
        outputs[0].astype(jnp.bfloat16), "ctx", scatter_dimension=0, tiled=True
    )
    returned = lax.all_to_all(expert_out, "exp", split_axis=0, concat_axis=0, tiled=True).reshape(
        slot_count, model_width
    )
    matches = target_index[:, :, None] == slot_iota[None, None, :]
    combine = jnp.sum(
        jnp.where(matches, route_weight[:, :, None], jnp.zeros_like(route_weight)[:, :, None]),
        axis=1,
    )
    moe_out = jnp.dot(combine, returned.astype(jnp.float32), precision=lax.Precision.HIGHEST)
    return (hidden_float + moe_out).astype(jnp.bfloat16)


def solution(mesh):
    placed = (
        P("ctx", "exp"),
        P("ctx", "exp"),
        P("ctx", "exp"),
        P(None, "ctx"),
        P(None, "ctx"),
        P(None, "exp"),
        P("exp"),
        P("exp", None),
        P(("ctx", "exp"), None),
        P(),
        P("exp", None, "ctx"),
        P("exp", None, "ctx"),
        P("exp", "ctx", None),
        P(("ctx", "exp"), None),
        P(("ctx", "exp"), None),
        P(("ctx", "exp"), None),
    )
    return jax.shard_map(
        on_device, mesh=mesh, in_specs=placed, out_specs=P(("ctx", "exp"), None), check_vma=False
    )
```

profile of v0, /device:TPU:0, one launch (start us, length us, event | category | flops | bytes accessed | tf_op | source)
XLA Modules:
  0.0 205.2 jit_solution(5551518412730478599)
XLA Ops:
  6.5 0.9 exponential_negate_fusion
  7.4 1.0 convert_bitcast_fusion
  8.4 1.3 fusion.20
  9.7 0.8 copy.27
  10.5 1.0 slice_bitcast_fusion.31
  11.6 0.8 copy.28
  12.4 13.4 %while.31 = (s32[]{:T(128)}, f32[16,1024]{1,0:T(8,128)S(1)}, f32[1024]{0:T(1024)S(1)}, f32[16,8,1024]{2,1,0:T(8,128)S(1)}, f32[16,8,1024]{2,1,0:T(8,128)S(1)}, /...) while((s32[]{:T(128)}, f32[16,1024]{1,0:T(8,128)S(1)}, ...), condition=%wide.region_9.10_spmd.clone, body=%wide.region_0.9_spmd.clone.sunk | while | flops 1156106 | bytes 1459865 | solution.py:63
  12.7 0.2 multiply_reduce_fusion.11
  12.8 0.1 multiply_reduce_fusion.13
  13.5 0.2 multiply_reduce_fusion.11
  13.7 0.1 multiply_reduce_fusion.13
  13.8 0.1 multiply_reduce_fusion.12
  14.3 0.2 multiply_reduce_fusion.11
  14.5 0.1 multiply_reduce_fusion.13
  14.6 0.1 multiply_reduce_fusion.12
  15.2 0.2 multiply_reduce_fusion.11
  15.3 0.1 multiply_reduce_fusion.13
  15.5 0.1 multiply_reduce_fusion.12
  16.0 0.2 multiply_reduce_fusion.11
  16.2 0.1 multiply_reduce_fusion.13
  16.3 0.1 multiply_reduce_fusion.12
  16.9 0.2 multiply_reduce_fusion.11
  17.0 0.1 multiply_reduce_fusion.13
  17.7 0.2 multiply_reduce_fusion.11
  17.9 0.1 multiply_reduce_fusion.13
  18.0 0.1 multiply_reduce_fusion.12
  18.5 0.2 multiply_reduce_fusion.11
  18.7 0.1 multiply_reduce_fusion.13
  18.8 0.1 multiply_reduce_fusion.12
  19.4 0.2 multiply_reduce_fusion.11
  19.5 0.1 multiply_reduce_fusion.13
  20.2 0.2 multiply_reduce_fusion.11
  20.4 0.1 multiply_reduce_fusion.13
  20.5 0.1 multiply_reduce_fusion.12
  21.0 0.2 multiply_reduce_fusion.11
  21.2 0.1 multiply_reduce_fusion.13
  21.4 0.1 multiply_reduce_fusion.12
  21.9 0.2 multiply_reduce_fusion.11
  22.1 0.1 multiply_reduce_fusion.13
  22.7 0.2 multiply_reduce_fusion.11
  22.9 0.1 multiply_reduce_fusion.13
  23.6 0.2 multiply_reduce_fusion.11
  23.7 0.1 multiply_reduce_fusion.13
  24.4 0.2 multiply_reduce_fusion.11
  24.6 0.1 multiply_reduce_fusion.13
  25.2 0.2 multiply_reduce_fusion.11
  25.4 0.1 multiply_reduce_fusion.13
  25.9 10.9 %all-gather = bf16[128,1024]{1,0:T(8,128)(2,1)S(1)} all-gather(bf16[16,1024]{1,0:T(8,128)(2,1)S(1)} %exponential_convert_fusion), channel_id=2, replica_groups=mesh['ctx'=8,'exp'=4] {'ctx'}, dimensions={0}, use_global_device_ids=true | all-gather | bytes 294912 | tf_op jit(solution)/shard_map/all_gather | solution.py:12
  36.8 9.3 %all-gather.1 = bf16[128,1024]{1,0:T(8,128)(2,1)S(1)} all-gather(bf16[16,1024]{1,0:T(8,128)(2,1)S(1)} %convert_element_type.70), channel_id=3, replica_groups=mesh['ctx'=8,'exp'=4] {'ctx'}, dimensions={0}, use_global_device_ids=true | all-gather | bytes 294912 | tf_op jit(solution)/shard_map/all_gather | solution.py:12
  46.1 0.4 while.32
  46.6 5.8 %convolution_convert_fusion = bf16[128,2048]{1,0:T(8,128)(2,1)} fusion(bf16[1024,2048]{1,0:T(8,128)(2,1)} %param.27, bf16[128,1024]{1,0:T(8,128)(2,1)S(1)} %copy-done, bf16[128,1024]{1,0:T(8,128)(2,1)S(1)} %copy-done.10, f32[16,8,1024]{2,1,0:T(8,128)S(1)} %get-tuple-element.155, f32[16,8,1024]{2,1,0:T(8,128)S(1)} %get-tuple-element.154, ...), kind=kOutput, calls=%fused_computation.64 | convolution fusion | flops 546832384 | bytes 6434816 | tf_op jit(solution)/shard_map/dot_general | solution.py:107
  52.6 38.6 %all-reduce.2.cloned.1.call-done = bf16[128,2048]{1,0:T(8,128)(2,1)} async-done(((bf16[128,2048]{1,0:T(8,128)(2,1)}), bf16[128,2048]{1,0:T(8,128)(2,1)}) %all-reduce.2.cloned.1.call-update) | async-done | bytes 524304 | tf_op jit(solution)/shard_map/psum | solution.py:110
  91.2 0.9 add_convert_fusion
  92.1 0.1 fusion.86
  92.3 0.3 convolution_convert_fusion.1
  92.6 11.4 %all_to_all.10 = bf16[4,16,2048]{2,1,0:T(8,128)(2,1)} all-to-all(bf16[4,16,2048]{2,1,0:T(8,128)(2,1)S(1)} %bitcast.443), channel_id=1, replica_groups=mesh['ctx'=8,'exp'=4] {'exp'}, dimensions={0} | all-to-all | bytes 524288 | tf_op jit(solution)/shard_map/all_to_all | solution.py:128
  104.0 27.2 %all-gather.4.cloned.1.call-done = bf16[32,16,2048]{2,1,0:T(8,128)(2,1)} async-done(((bf16[4,16,2048]{2,1,0:T(8,128)(2,1)}), bf16[32,16,2048]{2,1,0:T(8,128)(2,1)}) %all-gather.4.cloned.1.call-update) | async-done | bytes 2097168 | tf_op jit(solution)/shard_map/all_gather | solution.py:135
  131.2 5.3 %fusion.6 = f32[512,1024]{1,0:T(8,128)S(1)} fusion(bf16[512,2048]{1,0:T(8,128)(2,1)} %bitcast.513, bf16[1,2048,1024]{2,1,0:T(8,128)(2,1)} %param.30), kind=kOutput, calls=%fused_computation.61 | convolution fusion | flops 2147483648 | bytes 8388608 | tf_op jit(solution)/shard_map/dot_general | solution.py:139
  136.6 2.5 %multiply_convert_fusion = bf16[512,1024]{1,0:T(8,128)(2,1)S(1)} fusion(f32[512,1024]{1,0:T(8,128)S(1)} %fusion.6, bf16[512,2048]{1,0:T(8,128)(2,1)S(1)} %bitcast.514, bf16[1,2048,1024]{2,1,0:T(8,128)(2,1)S(1)} %copy-done.7), kind=kOutput, calls=%fused_computation.68 | convolution fusion | flops 2150629376 | bytes 9437184 | tf_op jit(solution)/shard_map/dot_general | solution.py:140
  139.1 3.7 %fusion.8 = bf16[32,16,2048]{2,1,0:T(8,128)(2,1)} fusion(bf16[32,16,1024]{2,1,0:T(8,128)(2,1)S(1)} %bitcast.515, bf16[1,1024,2048]{2,1,0:T(8,128)(2,1)S(1)} %copy-done.8), kind=kOutput, calls=%fused_computation.63 | convolution fusion | flops 2148532224 | bytes 7340032 | tf_op jit(solution)/shard_map/dot_general | solution.py:147
  142.8 41.4 %reduce-scatter.2.cloned.1.call-done = bf16[4,16,2048]{2,1,0:T(8,128)(2,1)} async-done(((bf16[32,16,2048]{2,1,0:T(8,128)(2,1)}), bf16[4,16,2048]{2,1,0:T(8,128)(2,1)}) %reduce-scatter.2.cloned.1.call-update) | async-done | bytes 262160 | tf_op jit(solution)/shard_map/reduce_scatter | solution.py:149
  184.2 4.6 %all-to-all-start.1 = ((bf16[4,16,2048]{2,1,0:T(8,128)(2,1)}), bf16[4,16,2048]{2,1,0:T(8,128)(2,1)S(1)}, u32[]{:S(2)}, u32[]{:S(2)}) async-start(bf16[4,16,2048]{2,1,0:T(8,128)(2,1)} %reduce-scatter.2.cloned.1.call-done), calls=%async_computation.2 | async-start | bytes 524288 | tf_op jit(solution)/shard_map/all_to_all | solution.py:152
  188.9 8.8 %all-to-all-done.1 = bf16[4,16,2048]{2,1,0:T(8,128)(2,1)S(1)} async-done(((bf16[4,16,2048]{2,1,0:T(8,128)(2,1)}), bf16[4,16,2048]{2,1,0:T(8,128)(2,1)S(1)}, u32[]{:S(2)}, u32[]{:S(2)}) %all-to-all-start.1) | async-done | bytes 262176 | tf_op jit(solution)/shard_map/all_to_all | solution.py:152
  197.7 0.9 fusion.11
  (235 shorter events, 6.6 us)
Async XLA Ops:
  6.5 84.7 %all-reduce.2.cloned.1.call-start = ((), (), s32[]{:S(2)}) async-start(), calls=%async_computation.3 | async-start | bytes 1048576 | tf_op jit(solution)/shard_map/psum | solution.py:110
  12.4 13.5 %copy-start.1 = (f32[16,1024]{1,0:T(8,128)S(1)}, f32[16,1024]{1,0:T(8,128)}, u32[]{:S(2)}) copy-start(f32[16,1024]{1,0:T(8,128)} %param.25) | copy-start | bytes 196612
  25.9 20.7 %copy-start = (bf16[128,1024]{1,0:T(8,128)(2,1)S(1)}, bf16[128,1024]{1,0:T(8,128)(2,1)}, u32[]{:S(2)}) copy-start(bf16[128,1024]{1,0:T(8,128)(2,1)} %param.20) | copy-start | bytes 786436
  25.9 20.7 %copy-start.10 = (bf16[128,1024]{1,0:T(8,128)(2,1)S(1)}, bf16[128,1024]{1,0:T(8,128)(2,1)}, u32[]{:S(2)}) copy-start(bf16[128,1024]{1,0:T(8,128)(2,1)} %param.21) | copy-start | bytes 786436
  25.9 20.7 %copy-start.11 = (f32[1024]{0:T(1024)S(1)}, f32[1024]{0:T(1024)}, u32[]{:S(2)}) copy-start(f32[1024]{0:T(1024)} %param.26) | copy-start | bytes 12292
  46.6 5.9 %copy-start.4 = (s32[32,2]{0,1:T(2,128)S(1)}, s32[32,2]{0,1:T(2,128)}, u32[]{:S(2)}) copy-start(s32[32,2]{0,1:T(2,128)} %param.34) | copy-start | bytes 772
  46.6 5.9 %copy-start.5 = (s32[32,2]{0,1:T(2,128)S(1)}, s32[32,2]{0,1:T(2,128)}, u32[]{:S(2)}) copy-start(s32[32,2]{0,1:T(2,128)} %param.33) | copy-start | bytes 772
  46.6 44.6 %copy-start.2 = (bf16[32,2048]{1,0:T(8,128)(2,1)S(1)}, bf16[32,2048]{1,0:T(8,128)(2,1)}, u32[]{:S(2)}) copy-start(bf16[32,2048]{1,0:T(8,128)(2,1)} %param.28) | copy-start | bytes 393220
  46.6 45.7 %copy-start.3 = (f32[2048]{0:T(1024)S(1)}, f32[2048]{0:T(1024)}, u32[]{:S(2)}) copy-start(f32[2048]{0:T(1024)} %param.29) | copy-start | bytes 24580
  52.5 78.8 %all-gather.4.cloned.1.call-start = ((), (), s32[]{:S(2)}) async-start(), calls=%async_computation.4 | async-start | bytes 2359296 | tf_op jit(solution)/shard_map/all_gather | solution.py:135
  104.0 80.2 %reduce-scatter.2.cloned.1.call-start = ((), (), s32[]{:S(2)}) async-start(), calls=%async_computation.5 | async-start | bytes 2359296 | tf_op jit(solution)/shard_map/reduce_scatter | solution.py:149
  131.2 5.3 %copy-start.7 = (bf16[1,2048,1024]{2,1,0:T(8,128)(2,1)S(1)}, bf16[1,2048,1024]{2,1,0:T(8,128)(2,1)}, u32[]{:S(2)}) copy-start(bf16[1,2048,1024]{2,1,0:T(8,128)(2,1)} %param.31) | copy-start | bytes 12582916
  131.2 5.3 %copy-start.9 = (bf16[32,16,2048]{2,1,0:T(8,128)(2,1)S(1)}, bf16[32,16,2048]{2,1,0:T(8,128)(2,1)}, u32[]{:S(2)}) copy-start(bf16[32,16,2048]{2,1,0:T(8,128)(2,1)} %all-gather.4.cloned.1.call-done) | copy-start | bytes 6291460
  136.6 2.5 %copy-start.8 = (bf16[1,1024,2048]{2,1,0:T(8,128)(2,1)S(1)}, bf16[1,1024,2048]{2,1,0:T(8,128)(2,1)}, u32[]{:S(2)}) copy-start(bf16[1,1024,2048]{2,1,0:T(8,128)(2,1)} %param.32) | copy-start | bytes 12582916
  142.8 46.0 %copy-start.6 = (f32[32,2]{0,1:T(2,128)S(1)}, f32[32,2]{0,1:T(2,128)}, u32[]{:S(2)}) copy-start(f32[32,2]{0,1:T(2,128)} %param.35) | copy-start | bytes 772
  184.2 13.5 %all-to-all-start.1 = ((bf16[4,16,2048]{2,1,0:T(8,128)(2,1)}), bf16[4,16,2048]{2,1,0:T(8,128)(2,1)S(1)}, u32[]{:S(2)}, u32[]{:S(2)}) async-start(bf16[4,16,2048]{2,1,0:T(8,128)(2,1)} %reduce-scatter.2.cloned.1.call-done), calls=%async_computation.2 | async-start | bytes 524288 | tf_op jit(solution)/shard_map/all_to_all | solution.py:152
Sparse Core Ops, SparseCore 0:
  52.6 38.5 all-reduce.1
  104.1 27.0 all-gather.3
  143.0 41.1 reduce-scatter.1
where the time goes:
time: 206 us; the launch traced here: 205 us
  waiting for transfers between devices  116 us (56%)
  blocking collectives  31.6 us (15%)
  matrix products  18.6 us (9%)
  between operations  13.4 us (7%)
  other arithmetic  12.1 us (6%)
  local copies, waits for them, and re-layouts  7.03 us (3%)
  starting transfers between devices  4.69 us (2%)
    reduce_scatter x1, waiting for transfers between devices, on_device(): lax.psum_scatter(outputs[0].astype(jnp.bfloat16), 'ctx', scatter_dimensio...  41.4 us
    psum x1, waiting for transfers between devices, on_device(): lax.psum(partial_out.astype(jnp.bfloat16), 'exp').astype(jnp.float32)  38.6 us
    all_gather x1, waiting for transfers between devices, on_device(): piece = lax.all_gather(arrived, 'ctx', axis=0, tiled=True)  27.2 us
    all_gather x2, blocking collectives, prefix(): lax.all_gather(part.astype(kind), axis)  20.2 us
    all_to_all x1, blocking collectives, on_device(): lax.all_to_all(dispatch.reshape(n_exp, per_device, model_width), 'exp', s...  11.4 us
    all_to_all x1, waiting for transfers between devices, on_device(): lax.all_to_all(expert_out, 'exp', split_axis=0, concat_axis=0, tiled=True)  8.81 us
    reduce_sum x48, other arithmetic, advance(): outputs.append(jnp.sum(c_blk[inner_pos][:, None] * state, axis=0))  6.82 us
    dot_general x1, matrix products, on_device(): partial_out = jnp.dot(gated, out_proj, preferred_element_type=jnp.float32)  5.81 us
  transfers between devices with their start and end apart: 4, of which 4 were waited for; matrix products, arithmetic and copies ran while one was open for 0% of the time, Pallas kernels for 0%

commit v1 on v0

--- a/solution.py
+++ b/solution.py
@@ -1,9 +1,405 @@
+import functools
+
 import jax
 import jax.numpy as jnp
 from jax import lax
+from jax.experimental import pallas as pl
+from jax.experimental.pallas import tpu as pltpu
 from jax.sharding import PartitionSpec as P
 
 EPSILON = 1e-05
+
+
+CORE, X, Y = 1, 2, 4
+MESH = pl.DeviceIdType.MESH
+
+
+class Links:
+    def __init__(self, send_sem):
+        self.ctx = lax.axis_index("ctx")
+        self.exp = lax.axis_index("exp")
+        self.send_sem = send_sem
+        self.sent = []
+
+    def copy(self, src, dst, recv_sem, device):
+        made = pltpu.make_async_remote_copy(
+            src_ref=src,
+            dst_ref=dst,
+            send_sem=self.send_sem.at[len(self.sent)],
+            recv_sem=recv_sem,
+            device_id=device,
+            device_id_type=MESH,
+        )
+        made.start()
+        self.sent.append(made)
+
+    def to_ctx(self, src, dst, recv_sem, mask):
+        self.copy(src, dst, recv_sem, (self.ctx ^ mask, self.exp))
+
+    def to_exp(self, src, dst, recv_sem, peer):
+        self.copy(src, dst, recv_sem, (self.ctx, peer))
+
+    def arrived(self, dst, recv_sem):
+        pltpu.make_async_remote_copy(
+            src_ref=dst,
+            dst_ref=dst,
+            send_sem=self.send_sem.at[0],
+            recv_sem=recv_sem,
+            device_id=(self.ctx ^ CORE, self.exp),
+            device_id_type=MESH,
+        ).wait_recv()
+
+    def finish(self):
+        for made in self.sent:
+            made.wait_send()
+
+
+def greet(links, n_exp):
+    barrier = pltpu.get_barrier_semaphore()
+    for mask in (CORE, X, Y):
+        pl.semaphore_signal(
+            barrier, inc=1, device_id=(links.ctx ^ mask, links.exp), device_id_type=MESH
+        )
+    for gap in range(1, n_exp):
+        pl.semaphore_signal(
+            barrier,
+            inc=1,
+            device_id=(links.ctx, lax.rem(links.exp + gap, n_exp)),
+            device_id_type=MESH,
+        )
+    pl.semaphore_wait(barrier, 3 + n_exp - 1)
+
+
+class Gather:
+    def __init__(self, links, slots, sems):
+        self.links, self.slots, self.sems = links, slots, sems
+        self.half = slots.shape[1] // 2
+
+    def part(self, mask, half):
+        return self.slots.at[mask, pl.ds(half * self.half, self.half)]
+
+    def send(self, mask, half, step):
+        self.links.to_ctx(
+            self.part(mask, half),
+            self.part(mask ^ step, half),
+            self.sems.at[mask ^ step, half],
+            step,
+        )
+
+    def wait(self, mask, half):
+        self.links.arrived(self.part(mask, half), self.sems.at[mask, half])
+
+    def begin(self, half):
+        for step in (X, Y, CORE):
+            self.send(0, half, step)
+
+    def forward_near(self):
+        self.wait(X, 0)
+        self.send(X, 0, Y)
+        self.send(X, 0, CORE)
+        self.wait(Y, 0)
+        self.send(Y, 0, CORE)
+        self.wait(Y, 1)
+        self.send(Y, 1, X)
+        self.send(Y, 1, CORE)
+        self.wait(X, 1)
+        self.send(X, 1, CORE)
+
+    def forward_far(self):
+        for half in range(2):
+            self.wait(X | Y, half)
+            self.send(X | Y, half, CORE)
+
+
+GATHER_SENDS = 14
+
+
+def prefix_kernel(local_ref, carried_ref, slots, send_sem, sems):
+    links = Links(send_sem)
+    greet(links, 1)
+    slots[0] = local_ref[...]
+    gather = Gather(links, slots, sems)
+    gather.begin(0)
+    gather.begin(1)
+    gather.forward_near()
+    gather.forward_far()
+    for mask in (1, 3, 5, 7):
+        gather.wait(mask, 0)
+        gather.wait(mask, 1)
+    states = carried_ref.shape[0]
+    state = jnp.zeros_like(carried_ref)
+    for k in range(7):
+        block = slots[links.ctx ^ k].astype(jnp.float32)
+        after = block[:states] * state + block[states:]
+        state = jnp.where(k < links.ctx, after, state)
+    carried_ref[...] = state
+    links.finish()
+
+
+def fast_prefix(through_final, final_state):
+    local = jnp.concatenate([through_final, final_state], axis=0).astype(jnp.bfloat16)
+    return pl.pallas_call(
+        prefix_kernel,
+        out_shape=jax.ShapeDtypeStruct(final_state.shape, jnp.float32),
+        in_specs=[pl.BlockSpec(memory_space=pltpu.VMEM)],
+        out_specs=pl.BlockSpec(memory_space=pltpu.VMEM),
+        scratch_shapes=[
+            pltpu.VMEM((8,) + local.shape, jnp.bfloat16),
+            pltpu.SemaphoreType.DMA((GATHER_SENDS,)),
+            pltpu.SemaphoreType.DMA((8, 2)),
+        ],
+        compiler_params=pltpu.CompilerParams(collective_id=1, has_side_effects=True),
+        cost_estimate=pl.CostEstimate(flops=10**6, bytes_accessed=10**6, transcendentals=0),
+    )(local)
+
+
+def expert_kernel(
+    n_exp,
+    partial_ref,
+    residual_ref,
+    gain_ref,
+    select_ref,
+    combine_ref,
+    gate_hbm,
+    up_hbm,
+    down_hbm,
+    out_ref,
+    gate_ref,
+    up_ref,
+    down_ref,
+    sums,
+    dispatch,
+    slots,
+    hidden,
+    products,
+    paired,
+    relay,
+    last,
+    total,
+    returned,
+    load_sem,
+    send_sem,
+    sum_sem,
+    dispatch_sem,
+    gather_sem,
+    pair_sem,
+    relay_sem,
+    last_sem,
+    return_sem,
+):
+    links = Links(send_sem)
+    tokens = residual_ref.shape[0]
+    cap = dispatch.shape[1]
+    half_rows = total.shape[0] // 2
+    halves = (pl.ds(0, half_rows), pl.ds(half_rows, half_rows))
+    exp = links.exp
+    loads = [
+        pltpu.make_async_copy(src.at[0], dst, load_sem.at[k])
+        for k, (src, dst) in enumerate(
+            ((gate_hbm, gate_ref), (up_hbm, up_ref), (down_hbm, down_ref))
+        )
+    ]
+    for load in loads:
+        load.start()
+    greet(links, n_exp)
+
+    for gap in range(1, n_exp):
+        peer = lax.rem(exp + gap, n_exp)
+        links.to_exp(
+            partial_ref.at[pl.ds(pl.multiple_of(peer * tokens, tokens), tokens)],
+            sums.at[gap - 1],
+            sum_sem.at[gap - 1],
+            peer,
+        )
+    mixer_out = partial_ref[pl.ds(pl.multiple_of(exp * tokens, tokens), tokens), :].astype(
+        jnp.float32
+    )
+    for gap in range(1, n_exp):
+        links.arrived(sums.at[gap - 1], sum_sem.at[gap - 1])
+        mixer_out = mixer_out + sums[gap - 1].astype(jnp.float32)
+    hidden_one = (residual_ref[...].astype(jnp.float32) + mixer_out).astype(jnp.bfloat16)
+    hidden_float = hidden_one.astype(jnp.float32)
+    inv_rms = lax.rsqrt(jnp.mean(hidden_float * hidden_float, axis=-1, keepdims=True) + EPSILON)
+    normed = (hidden_float * inv_rms * gain_ref[...]).astype(jnp.bfloat16)
+    rows = jnp.dot(select_ref[...], normed, preferred_element_type=jnp.float32)
+    dispatch[...] = rows.astype(jnp.bfloat16).reshape(dispatch.shape)
+
+    def rows_of(gap):
+        return slots.at[0, pl.ds(gap * cap, cap)]
+
+    for gap in range(1, n_exp):
+        peer = lax.rem(exp + gap, n_exp)
+        links.to_exp(dispatch.at[peer], rows_of(gap), dispatch_sem.at[gap - 1], peer)
+    slots[0, 0:cap] = dispatch[exp]
+    gather = Gather(links, slots, gather_sem)
+    for half in range(2):
+        for gap in range(half * n_exp // 2, (half + 1) * n_exp // 2):
+            if gap:
+                links.arrived(rows_of(gap), dispatch_sem.at[gap - 1])
+        gather.begin(half)
+    gather.forward_near()
+
+    tile = 256
+    group = 4
+
+    def experts(first):
+        count = group * slots.shape[1]
+
+        @pl.loop(0, gate_ref.shape[1] // tile)
+        def _(j):
+            columns = pl.ds(pl.multiple_of(j * tile, tile), tile)
+            x = slots[first : first + group].reshape(count, slots.shape[2])
+            gate = jnp.dot(x, gate_ref[:, columns], preferred_element_type=jnp.float32)
+            up = jnp.dot(x, up_ref[:, columns], preferred_element_type=jnp.float32)
+            hidden[:, columns] = (jax.nn.silu(gate) * up).astype(jnp.bfloat16)
+
+        @pl.loop(0, down_ref.shape[1] // tile)
+        def _(j):
+            columns = pl.ds(pl.multiple_of(j * tile, tile), tile)
+            y = jnp.dot(hidden[...], down_ref[:, columns], preferred_element_type=jnp.float32)
+            products[first : first + group, :, columns] = y.astype(jnp.bfloat16).reshape(
+                group, slots.shape[1], tile
+            )
+
+    def pair(mask):
+        at = (mask ^ CORE) // 2
+        links.to_ctx(products.at[mask], paired.at[at], pair_sem.at[at], CORE)
+
+    for mask in (1, 3):
+        gather.wait(mask, 0)
+        gather.wait(mask, 1)
+    for load in loads:
+        load.wait()
+    experts(0)
+    gather.forward_far()
+    pair(1)
+    pair(3)
+    for mask in (5, 7):
+        gather.wait(mask, 0)
+        gather.wait(mask, 1)
+    experts(4)
+    pair(7)
+    pair(5)
+
+    def both(mask, rows):
+        return products[mask, rows].astype(jnp.float32) + paired[mask // 2, rows].astype(
+            jnp.float32
+        )
+
+    def store(mask, rows, value):
+        products[mask, rows] = value.astype(jnp.bfloat16)
+
+    far = X | Y
+    links.arrived(paired.at[far // 2], pair_sem.at[far // 2])
+    for half, step in ((0, Y), (1, X)):
+        store(far, halves[half], both(far, halves[half]))
+        links.to_ctx(products.at[far, halves[half]], relay.at[half], relay_sem.at[half], step)
+
+    def onward(at, step, half):
+        links.to_ctx(
+            products.at[step, halves[half]],
+            last.at[at, halves[half]],
+            last_sem.at[at, half],
+            step,
+        )
+
+    for at, step in ((0, X), (1, Y)):
+        half = 1 - at
+        links.arrived(paired.at[step // 2], pair_sem.at[step // 2])
+        store(step, halves[half], both(step, halves[half]))
+        onward(at, step, half)
+    for at, step in ((0, X), (1, Y)):
+        half = at
+        links.arrived(relay.at[half], relay_sem.at[half])
+        store(step, halves[half], both(step, halves[half]) + relay[half].astype(jnp.float32))
+        onward(at, step, half)
+    links.arrived(paired.at[0], pair_sem.at[0])
+    for half in range(2):
+        value = both(0, halves[half])
+        for at in range(2):
+            links.arrived(last.at[at, halves[half]], last_sem.at[at, half])
+            value = value + last[at, halves[half]].astype(jnp.float32)
+        total[halves[half]] = value.astype(jnp.bfloat16)
+        for gap in range(half * n_exp // 2, (half + 1) * n_exp // 2):
+            mine = total.at[pl.ds(gap * cap, cap)]
+            if gap:
+                links.to_exp(
+                    mine,
+                    returned.at[exp],
+                    return_sem.at[gap - 1],
+                    lax.rem(exp + n_exp - gap, n_exp),
+                )
+            else:
+                returned[exp] = mine[...]
+    for gap in range(1, n_exp):
+        links.arrived(returned.at[lax.rem(exp + gap, n_exp)], return_sem.at[gap - 1])
+    picked = returned[...].reshape(n_exp * cap, returned.shape[2]).astype(jnp.float32)
+    moe_out = jnp.dot(
+        combine_ref[...],
+        picked,
+        precision=lax.Precision.HIGHEST,
+        preferred_element_type=jnp.float32,
+    )
+    out_ref[...] = (hidden_float + moe_out).astype(jnp.bfloat16)
+    links.finish()
+
+
+def fast_experts(
+    partial_out, residual, norm_gain, select, combine, gate_proj, up_proj, down_proj, n_exp, cap
+):
+    tokens, width = residual.shape
+    rows = n_exp * cap
+    bf16 = jnp.bfloat16
+    dma = pltpu.SemaphoreType.DMA
+    vmem = pl.BlockSpec(memory_space=pltpu.VMEM)
+    sends = 3 * (n_exp - 1) + GATHER_SENDS + 4 + 2 + 4
+    return pl.pallas_call(
+        functools.partial(expert_kernel, n_exp),
+        out_shape=jax.ShapeDtypeStruct((tokens, width), bf16),
+        in_specs=[vmem] * 5 + [pl.BlockSpec(memory_space=pl.ANY)] * 3,
+        out_specs=vmem,
+        scratch_shapes=[
+            pltpu.VMEM(gate_proj.shape[1:], bf16),
+            pltpu.VMEM(up_proj.shape[1:], bf16),
+            pltpu.VMEM(down_proj.shape[1:], bf16),
+            pltpu.VMEM((n_exp - 1, tokens, width), bf16),
+            pltpu.VMEM((n_exp, cap, width), bf16),
+            pltpu.VMEM((8, rows, width), bf16),
+            pltpu.VMEM((4 * rows, gate_proj.shape[2]), bf16),
+            pltpu.VMEM((8, rows, width), bf16),
+            pltpu.VMEM((4, rows, width), bf16),
+            pltpu.VMEM((2, rows // 2, width), bf16),
+            pltpu.VMEM((2, rows, width), bf16),
+            pltpu.VMEM((rows, width), bf16),
+            pltpu.VMEM((n_exp, cap, width), bf16),
+            dma((3,)),
+            dma((sends,)),
+            dma((n_exp - 1,)),
+            dma((n_exp - 1,)),
+            dma((8, 2)),
+            dma((4,)),
+            dma((2,)),
+            dma((2, 2)),
+            dma((n_exp - 1,)),
+        ],
+        compiler_params=pltpu.CompilerParams(
+            collective_id=2, has_side_effects=True, vmem_limit_bytes=48 * 1024 * 1024
+        ),
+        cost_estimate=pl.CostEstimate(
+            flops=6 * 8 * rows * width * gate_proj.shape[2],
+            bytes_accessed=6 * width * gate_proj.shape[2],
+            transcendentals=0,
+        ),
+    )(
+        partial_out,
+        residual,
+        norm_gain.reshape(1, width),
+        select,
+        combine,
+        gate_proj,
+        up_proj,
+        down_proj,
+    )
 
 
 def prefix(array, axis, combine, identity):
@@ -93,8 +489,22 @@
     )
     through_final = jnp.exp(total_step[None, :] * decay_rate)
     identity = (jnp.ones_like(through_final), jnp.zeros_like(final_state))
-    carried = prefix((through_final, final_state), "ctx", link_states, identity)
-    carried_state = carried[1]
+    tok_dev = residual.shape[0]
+    model_width = residual.shape[1]
+    experts_local = gate_proj.shape[0]
+    experts_all = experts_local * n_exp
+    capacity = max(2, expert_ids.shape[1] * tok_dev // experts_all)
+    cube = (
+        lax.axis_size("ctx") == 8
+        and n_exp == 4
+        and experts_local == 1
+        and capacity % 16 == 0
+        and tok_dev % 16 == 0
+    )
+    if cube:
+        carried_state = fast_prefix(through_final, final_state)
+    else:
+        carried_state = prefix((through_final, final_state), "ctx", link_states, identity)[1]
     correction = jnp.zeros_like(local_y)
     for state_index in range(decay_rate.shape[0]):
         weight_row = (
@@ -105,8 +515,31 @@
     mixer_y = local_y + correction + skip_gain * x_float
     gated = (mixer_y * jax.nn.silu(mixer_z.astype(jnp.float32))).astype(jnp.bfloat16)
     partial_out = jnp.dot(gated, out_proj, preferred_element_type=jnp.float32)
-    tok_dev = residual.shape[0]
-    model_width = residual.shape[1]
+    slot_count = experts_all * capacity
+    per_device = experts_local * capacity
+    target_index = jnp.where(slot_ids >= 0, expert_ids * capacity + slot_ids, -1)
+    slot_iota = jnp.arange(slot_count, dtype=jnp.int32)
+    select = jnp.any(target_index[None, :, :] == slot_iota[:, None, None], axis=-1).astype(
+        jnp.bfloat16
+    )
+    matches = target_index[:, :, None] == slot_iota[None, None, :]
+    combine = jnp.sum(
+        jnp.where(matches, route_weight[:, :, None], jnp.zeros_like(route_weight)[:, :, None]),
+        axis=1,
+    )
+    if cube:
+        return fast_experts(
+            partial_out.astype(jnp.bfloat16),
+            residual,
+            norm_gain,
+            select,
+            combine,
+            gate_proj,
+            up_proj,
+            down_proj,
+            n_exp,
+            capacity,
+        )
     summed = lax.psum(partial_out.astype(jnp.bfloat16), "exp").astype(jnp.float32)
     mixer_out = lax.dynamic_slice_in_dim(summed, lax.axis_index("exp") * tok_dev, tok_dev, 0)
     hidden_one = (residual.astype(jnp.float32) + mixer_out).astype(jnp.bfloat16)
@@ -114,16 +547,6 @@
     hidden_float = hidden_one.astype(jnp.float32)
     inv_rms = lax.rsqrt(jnp.mean(hidden_float * hidden_float, axis=-1, keepdims=True) + EPSILON)
     normed = (hidden_float * inv_rms * norm_gain).astype(jnp.bfloat16)
-    experts_local = gate_proj.shape[0]
-    experts_all = experts_local * n_exp
-    capacity = max(2, expert_ids.shape[1] * tok_dev // experts_all)
-    slot_count = experts_all * capacity
-    per_device = experts_local * capacity
-    target_index = jnp.where(slot_ids >= 0, expert_ids * capacity + slot_ids, -1)
-    slot_iota = jnp.arange(slot_count, dtype=jnp.int32)
-    select = jnp.any(target_index[None, :, :] == slot_iota[:, None, None], axis=-1).astype(
-        jnp.bfloat16
-    )
     dispatch = jnp.dot(select, normed, preferred_element_type=jnp.float32).astype(jnp.bfloat16)
     arrived = lax.all_to_all(
         dispatch.reshape(n_exp, per_device, model_width),
@@ -151,11 +574,6 @@
     )
     returned = lax.all_to_all(expert_out, "exp", split_axis=0, concat_axis=0, tiled=True).reshape(
         slot_count, model_width
-    )
-    matches = target_index[:, :, None] == slot_iota[None, None, :]
-    combine = jnp.sum(
-        jnp.where(matches, route_weight[:, :, None], jnp.zeros_like(route_weight)[:, :, None]),
-        axis=1,
     )
     moe_out = jnp.dot(combine, returned.astype(jnp.float32), precision=lax.Precision.HIGHEST)
     return (hidden_float + moe_out).astype(jnp.bfloat16)

time: 206 us -> 105 us (0.51)
  waiting for transfers between devices: 116 us -> 0 us
  Pallas kernels: 0 us -> 75.6 us
  blocking collectives: 31.6 us -> 0 us
  matrix products: 18.6 us -> 4.9 us
  between operations: 13.4 us -> 0.3 us
  starting transfers between devices: 4.69 us -> 0 us
  local copies, waits for them, and re-layouts: 7.03 us -> 10.2 us
    pallas_call x0 -> x2, Pallas kernels: none -> 75.6 us  [the longest x1 63.9 us: fast_experts(): pl.pallas_call(functools.partial(expert_kernel, n_exp), out_shape=jax.Sha...]
    reduce_scatter x1 -> x0, waiting for transfers between devices: 41.4 us -> none  [on_device(): lax.psum_scatter(outputs[0].astype(jnp.bfloat16), 'ctx', scatter_dimensio...]
    psum x1 -> x0, waiting for transfers between devices: 38.6 us -> none  [on_device(): lax.psum(partial_out.astype(jnp.bfloat16), 'exp').astype(jnp.float32)]
    all_gather x1 -> x0, waiting for transfers between devices: 27.2 us -> none  [on_device(): piece = lax.all_gather(arrived, 'ctx', axis=0, tiled=True)]
    all_gather x2 -> x0, blocking collectives: 20.2 us -> none  [prefix(): lax.all_gather(part.astype(kind), axis)]
    dot_general x5 -> x0, matrix products: 12.7 us -> none  [the longest x1 5.29 us: on_device(): jnp.dot(rows_here, gate_proj[local_index], preferred_element_type=jnp.flo...]
    all_to_all x1 -> x0, blocking collectives: 11.4 us -> none  [on_device(): lax.all_to_all(dispatch.reshape(n_exp, per_device, model_width), 'exp', s...]
    all_to_all x1 -> x0, waiting for transfers between devices: 8.81 us -> none  [on_device(): lax.all_to_all(expert_out, 'exp', split_axis=0, concat_axis=0, tiled=True)]
  transfers between devices with their start and end apart: 4 -> 0, of which waited for: 4 -> 0; matrix products, arithmetic and copies ran while one was open for 0% -> 0% of each run, Pallas kernels for 0% -> 0%
where the time goes in v1:
time: 105 us; the launch traced here: 104 us
  Pallas kernels  75.6 us (72%)
  other arithmetic  11.5 us (11%)
  local copies, waits for them, and re-layouts  10.2 us (10%)
  matrix products  4.9 us (5%)
  loops' own time  1.66 us (2%)
    pallas_call x1, Pallas kernels, fast_experts(): pl.pallas_call(functools.partial(expert_kernel, n_exp), out_shape=jax.Sha...  63.9 us
    pallas_call x1, Pallas kernels, fast_prefix(): pl.pallas_call(prefix_kernel, out_shape=jax.ShapeDtypeStruct(final_state....  11.7 us
    reduce_sum x48, other arithmetic, advance(): outputs.append(jnp.sum(c_blk[inner_pos][:, None] * state, axis=0))  6.8 us
    dot_general x1, matrix products, on_device(): partial_out = jnp.dot(gated, out_proj, preferred_element_type=jnp.float32)  4.9 us
    unnamed x23, local copies, waits for them, and re-layouts  2.9 us

profile of v1, /device:TPU:0, one launch (start us, length us, event | category | flops | bytes accessed | tf_op | source)
XLA Modules:
  0.0 104.1 jit_solution(4374456503824558945)
XLA Ops:
  0.0 0.9 exponential_negate_fusion
  0.9 1.0 convert_bitcast_fusion
  1.9 1.3 %fusion.7 = f32[16,8,1024]{2,1,0:T(8,128)S(1)} fusion(f32[128,1024]{1,0:T(8,128)} %param.20), kind=kLoop, calls=%fused_computation.66 | loop fusion | flops 786432 | bytes 1048576 | tf_op jit(solution)/shard_map/reshape | solution.py:437
  3.2 0.8 copy.25
  4.0 0.8 copy.26
  4.9 13.4 %while.17 = (s32[]{:T(128)}, f32[16,1024]{1,0:T(8,128)S(1)}, f32[1024]{0:T(1024)S(1)}, f32[16,8,1024]{2,1,0:T(8,128)S(1)}, f32[16,8,1024]{2,1,0:T(8,128)S(1)}, /...) while((s32[]{:T(128)}, f32[16,1024]{1,0:T(8,128)S(1)}, ...), condition=%wide.region_9.10_spmd.clone, body=%wide.region_0.9_spmd.clone.sunk | while | flops 1156106 | bytes 1459865 | solution.py:459
  5.1 0.2 multiply_reduce_fusion.11
  5.3 0.1 multiply_reduce_fusion.13
  5.4 0.1 multiply_reduce_fusion.12
  5.9 0.2 multiply_reduce_fusion.11
  6.1 0.1 multiply_reduce_fusion.13
  6.3 0.1 multiply_reduce_fusion.12
  6.8 0.2 multiply_reduce_fusion.11
  7.0 0.1 multiply_reduce_fusion.13
  7.1 0.1 multiply_reduce_fusion.12
  7.6 0.2 multiply_reduce_fusion.11
  7.8 0.1 multiply_reduce_fusion.13
  7.9 0.1 multiply_reduce_fusion.12
  8.5 0.2 multiply_reduce_fusion.11
  8.6 0.1 multiply_reduce_fusion.13
  8.8 0.1 multiply_reduce_fusion.12
  9.3 0.2 multiply_reduce_fusion.11
  9.5 0.1 multiply_reduce_fusion.13
  9.6 0.1 multiply_reduce_fusion.12
  10.1 0.2 multiply_reduce_fusion.11
  10.3 0.1 multiply_reduce_fusion.13
  10.4 0.1 multiply_reduce_fusion.12
  11.0 0.2 multiply_reduce_fusion.11
  11.1 0.1 multiply_reduce_fusion.13
  11.3 0.1 multiply_reduce_fusion.12
  11.8 0.2 multiply_reduce_fusion.11
  12.0 0.1 multiply_reduce_fusion.13
  12.1 0.1 multiply_reduce_fusion.12
  12.6 0.2 multiply_reduce_fusion.11
  12.8 0.1 multiply_reduce_fusion.13
  13.0 0.1 multiply_reduce_fusion.12
  13.5 0.2 multiply_reduce_fusion.11
  13.7 0.1 multiply_reduce_fusion.13
  13.8 0.1 multiply_reduce_fusion.12
  14.3 0.2 multiply_reduce_fusion.11
  14.5 0.1 multiply_reduce_fusion.13
  14.6 0.1 multiply_reduce_fusion.12
  15.2 0.2 multiply_reduce_fusion.11
  15.3 0.1 multiply_reduce_fusion.13
  15.5 0.1 multiply_reduce_fusion.12
  16.0 0.2 multiply_reduce_fusion.11
  16.2 0.1 multiply_reduce_fusion.13
  16.3 0.1 multiply_reduce_fusion.12
  16.8 0.2 multiply_reduce_fusion.11
  17.0 0.1 multiply_reduce_fusion.13
  17.1 0.1 multiply_reduce_fusion.12
  17.7 0.2 multiply_reduce_fusion.11
  17.8 0.1 multiply_reduce_fusion.13
  18.0 0.1 multiply_reduce_fusion.12
  18.3 0.6 pad_maximum_fusion.local_ref
  19.0 11.7 %shard_map.154 = f32[16,1024]{1,0:T(8,128)} custom-call(bf16[32,1024]{1,0:T(8,128)(2,1)} %pad_maximum_fusion.local_ref), custom_call_target="tpu_custom_call" | custom-call | flops 1000000 | bytes 1000000 | tf_op jit(solution)/shard_map/pallas_call | solution.py:141
  30.7 1.3 %fusion.127 = (f32[1,1024]{1,0:T(1,128)S(1)}, f32[1,1024]{1,0:T(1,128)S(1)}, f32[1,1024]{1,0:T(1,128)S(1)}, f32[1,1024]{1,0:T(1,128)S(1)}, f32[1,1024]{1,0:T(1,1...) fusion(f32[16,1024]{1,0:T(8,128)} %shard_map.154), kind=kLoop, calls=%fused_computation.224 | loop fusion | bytes 131072 | tf_op jit(solution)/shard_map/slice | solution.py:512
  32.2 4.9 %convolution_convert_fusion.partial_ref = bf16[128,2048]{1,0:T(8,128)(2,1)S(1)} fusion(bf16[1024,2048]{1,0:T(8,128)(2,1)} %param.25, bf16[128,1024]{1,0:T(8,128)(2,1)S(1)} %copy-done.3, bf16[128,1024]{1,0:T(8,128)(2,1)S(1)} %copy-done.9, f32[16,8,1024]{2,1,0:T(8,128)S(1)} %get-tuple-element.61, f32[16,8,1024]{2,1,0:T(8,128)S(1)} %get-tuple-element.60, ...), kind=kOutput, calls=%fused_computation.54 | convolution fusion | flops 546832384 | bytes 6434816 | tf_op jit(solution)/shard_map/dot_general | solution.py:517
  37.1 0.1 fusion.123
  37.2 0.1 copy.27.select_ref
  37.3 0.1 select_reduce_fusion.combine_ref
  37.4 2.2 %copy-done = bf16[1,2048,1024]{2,1,0:T(8,128)(2,1)S(1)} copy-done((bf16[1,2048,1024]{2,1,0:T(8,128)(2,1)S(1)}, bf16[1,2048,1024]{2,1,0:T(8,128)(2,1)}, u32[]{:S(2)}) %copy-start) | copy-done | bytes 4194328
  39.6 63.9 %shard_map.155 = bf16[32,2048]{1,0:T(8,128)(2,1)S(1)} custom-call(bf16[128,2048]{1,0:T(8,128)(2,1)S(1)} %convolution_convert_fusion.partial_ref, bf16[32,2048]{1,0:T(8,128)(2,1)S(1)} %copy-done.1, f32[1,2048]{1,0:T(1,128)S(1)} %bitcast.393, bf16[64,32]{1,0:T(8,128)(2,1)S(1)} %copy.27.select_ref, f32[32,64]{1,0:T(8,128)S(1)} %select_reduce_fusion.combine_ref, ...), custom_call_target="tpu_custom_call" | custom-call | flops 6442450944 | bytes 12582912 | tf_op jit(solution)/shard_map/pallas_call | solution.py:356
  103.5 0.7 copy.46
  (207 shorter events, 5.1 us)
Async XLA Ops:
  4.8 13.5 %copy-start.4 = (f32[16,1024]{1,0:T(8,128)S(1)}, f32[16,1024]{1,0:T(8,128)}, u32[]{:S(2)}) copy-start(f32[16,1024]{1,0:T(8,128)} %param.23) | copy-start | bytes 196612
  4.8 27.2 %copy-start.5 = (f32[16,128]{1,0:T(8,128)S(1)}, f32[16,128]{1,0:T(8,128)}, u32[]{:S(2)}) copy-start(f32[16,128]{1,0:T(8,128)} %param.22) | copy-start | bytes 24580
  4.8 27.2 %copy-start.3 = (bf16[128,1024]{1,0:T(8,128)(2,1)S(1)}, bf16[128,1024]{1,0:T(8,128)(2,1)}, u32[]{:S(2)}) copy-start(bf16[128,1024]{1,0:T(8,128)(2,1)} %param.18) | copy-start | bytes 786436
  4.8 27.2 %copy-start.9 = (bf16[128,1024]{1,0:T(8,128)(2,1)S(1)}, bf16[128,1024]{1,0:T(8,128)(2,1)}, u32[]{:S(2)}) copy-start(bf16[128,1024]{1,0:T(8,128)(2,1)} %param.19) | copy-start | bytes 786436
  4.9 27.2 %copy-start.10 = (f32[1024]{0:T(1024)S(1)}, f32[1024]{0:T(1024)}, u32[]{:S(2)}) copy-start(f32[1024]{0:T(1024)} %param.24) | copy-start | bytes 12292
  32.1 5.0 %copy-start.6 = (s32[32,2]{0,1:T(2,128)S(1)}, s32[32,2]{0,1:T(2,128)}, u32[]{:S(2)}) copy-start(s32[32,2]{0,1:T(2,128)} %param.32) | copy-start | bytes 772
  32.1 5.0 %copy-start.7 = (s32[32,2]{0,1:T(2,128)S(1)}, s32[32,2]{0,1:T(2,128)}, u32[]{:S(2)}) copy-start(s32[32,2]{0,1:T(2,128)} %param.31) | copy-start | bytes 772
  32.1 5.2 %copy-start.8 = (f32[32,2]{0,1:T(2,128)S(1)}, f32[32,2]{0,1:T(2,128)}, u32[]{:S(2)}) copy-start(f32[32,2]{0,1:T(2,128)} %param.33) | copy-start | bytes 772
  32.1 5.3 %copy-start.1 = (bf16[32,2048]{1,0:T(8,128)(2,1)S(1)}, bf16[32,2048]{1,0:T(8,128)(2,1)}, u32[]{:S(2)}) copy-start(bf16[32,2048]{1,0:T(8,128)(2,1)} %residual_ref.1) | copy-start | bytes 393220
  32.2 5.3 %copy-start.2 = (f32[2048]{0:T(1024)S(1)}, f32[2048]{0:T(1024)}, u32[]{:S(2)}) copy-start(f32[2048]{0:T(1024)} %param.27) | copy-start | bytes 24580
  37.4 2.2 %copy-start = (bf16[1,2048,1024]{2,1,0:T(8,128)(2,1)S(1)}, bf16[1,2048,1024]{2,1,0:T(8,128)(2,1)}, u32[]{:S(2)}) copy-start(bf16[1,2048,1024]{2,1,0:T(8,128)(2,1)} %gate_hbm.1) | copy-start | bytes 12582916

commit v2 on v1

--- a/solution.py
+++ b/solution.py
@@ -112,6 +112,7 @@
 
 
 GATHER_SENDS = 14
+CHUNKS = 4
 
 
 def prefix_kernel(local_ref, carried_ref, slots, send_sem, sems):
@@ -155,15 +156,19 @@
 
 def expert_kernel(
     n_exp,
-    partial_ref,
+    gated_ref,
     residual_ref,
     gain_ref,
     select_ref,
     combine_ref,
+    proj_hbm,
     gate_hbm,
     up_hbm,
     down_hbm,
     out_ref,
+    proj_ref,
+    partial,
+    hidden_one,
     gate_ref,
     up_ref,
     down_ref,
@@ -177,6 +182,7 @@
     last,
     total,
     returned,
+    proj_sem,
     load_sem,
     send_sem,
     sum_sem,
@@ -193,32 +199,45 @@
     half_rows = total.shape[0] // 2
     halves = (pl.ds(0, half_rows), pl.ds(half_rows, half_rows))
     exp = links.exp
+    chunk = partial.shape[1] // CHUNKS
+    column_chunks = [pl.ds(k * chunk, chunk) for k in range(CHUNKS)]
+    proj_loads = [
+        pltpu.make_async_copy(proj_hbm.at[:, columns], proj_ref.at[:, columns], proj_sem.at[k])
+        for k, columns in enumerate(column_chunks)
+    ]
     loads = [
         pltpu.make_async_copy(src.at[0], dst, load_sem.at[k])
         for k, (src, dst) in enumerate(
             ((gate_hbm, gate_ref), (up_hbm, up_ref), (down_hbm, down_ref))
         )
     ]
-    for load in loads:
+    for load in proj_loads + loads:
         load.start()
     greet(links, n_exp)
 
-    for gap in range(1, n_exp):
-        peer = lax.rem(exp + gap, n_exp)
-        links.to_exp(
-            partial_ref.at[pl.ds(pl.multiple_of(peer * tokens, tokens), tokens)],
-            sums.at[gap - 1],
-            sum_sem.at[gap - 1],
-            peer,
-        )
-    mixer_out = partial_ref[pl.ds(pl.multiple_of(exp * tokens, tokens), tokens), :].astype(
-        jnp.float32
-    )
-    for gap in range(1, n_exp):
-        links.arrived(sums.at[gap - 1], sum_sem.at[gap - 1])
-        mixer_out = mixer_out + sums[gap - 1].astype(jnp.float32)
-    hidden_one = (residual_ref[...].astype(jnp.float32) + mixer_out).astype(jnp.bfloat16)
-    hidden_float = hidden_one.astype(jnp.float32)
+    def token_rows(peer):
+        return pl.ds(pl.multiple_of(peer * tokens, tokens), tokens)
+
+    for k, columns in enumerate(column_chunks):
+        proj_loads[k].wait()
+        part = jnp.dot(gated_ref[...], proj_ref[:, columns], preferred_element_type=jnp.float32)
+        partial[:, columns] = part.astype(jnp.bfloat16)
+        for gap in range(1, n_exp):
+            peer = lax.rem(exp + gap, n_exp)
+            links.to_exp(
+                partial.at[token_rows(peer), columns],
+                sums.at[gap - 1, :, columns],
+                sum_sem.at[gap - 1, k],
+                peer,
+            )
+    for k, columns in enumerate(column_chunks):
+        mixer_out = partial[token_rows(exp), columns].astype(jnp.float32)
+        for gap in range(1, n_exp):
+            links.arrived(sums.at[gap - 1, :, columns], sum_sem.at[gap - 1, k])
+            mixer_out = mixer_out + sums[gap - 1, :, columns].astype(jnp.float32)
+        mixed = residual_ref[:, columns].astype(jnp.float32) + mixer_out
+        hidden_one[:, columns] = mixed.astype(jnp.bfloat16)
+    hidden_float = hidden_one[...].astype(jnp.float32)
     inv_rms = lax.rsqrt(jnp.mean(hidden_float * hidden_float, axis=-1, keepdims=True) + EPSILON)
     normed = (hidden_float * inv_rms * gain_ref[...]).astype(jnp.bfloat16)
     rows = jnp.dot(select_ref[...], normed, preferred_element_type=jnp.float32)
@@ -242,8 +261,10 @@
     tile = 256
     group = 4
 
-    def experts(first):
-        count = group * slots.shape[1]
+    count = group * slots.shape[1]
+
+    def into_hidden(first):
+        at = pl.ds(first * slots.shape[1], count)
 
         @pl.loop(0, gate_ref.shape[1] // tile)
         def _(j):
@@ -251,12 +272,15 @@
             x = slots[first : first + group].reshape(count, slots.shape[2])
             gate = jnp.dot(x, gate_ref[:, columns], preferred_element_type=jnp.float32)
             up = jnp.dot(x, up_ref[:, columns], preferred_element_type=jnp.float32)
-            hidden[:, columns] = (jax.nn.silu(gate) * up).astype(jnp.bfloat16)
+            hidden[at, columns] = (jax.nn.silu(gate) * up).astype(jnp.bfloat16)
+
+    def out_of_hidden(first):
+        at = pl.ds(first * slots.shape[1], count)
 
         @pl.loop(0, down_ref.shape[1] // tile)
         def _(j):
             columns = pl.ds(pl.multiple_of(j * tile, tile), tile)
-            y = jnp.dot(hidden[...], down_ref[:, columns], preferred_element_type=jnp.float32)
+            y = jnp.dot(hidden[at, :], down_ref[:, columns], preferred_element_type=jnp.float32)
             products[first : first + group, :, columns] = y.astype(jnp.bfloat16).reshape(
                 group, slots.shape[1], tile
             )
@@ -270,16 +294,18 @@
         gather.wait(mask, 1)
     for load in loads:
         load.wait()
-    experts(0)
+    into_hidden(0)
     gather.forward_far()
-    pair(1)
-    pair(3)
     for mask in (5, 7):
         gather.wait(mask, 0)
         gather.wait(mask, 1)
-    experts(4)
+    into_hidden(4)
+    out_of_hidden(4)
     pair(7)
     pair(5)
+    out_of_hidden(0)
+    pair(3)
+    pair(1)
 
     def both(mask, rows):
         return products[mask, rows].astype(jnp.float32) + paired[mask // 2, rows].astype(
@@ -340,41 +366,55 @@
         precision=lax.Precision.HIGHEST,
         preferred_element_type=jnp.float32,
     )
-    out_ref[...] = (hidden_float + moe_out).astype(jnp.bfloat16)
+    out_ref[...] = (hidden_one[...].astype(jnp.float32) + moe_out).astype(jnp.bfloat16)
     links.finish()
 
 
 def fast_experts(
-    partial_out, residual, norm_gain, select, combine, gate_proj, up_proj, down_proj, n_exp, cap
+    gated,
+    residual,
+    norm_gain,
+    select,
+    combine,
+    out_proj,
+    gate_proj,
+    up_proj,
+    down_proj,
+    n_exp,
+    cap,
 ):
     tokens, width = residual.shape
     rows = n_exp * cap
     bf16 = jnp.bfloat16
     dma = pltpu.SemaphoreType.DMA
     vmem = pl.BlockSpec(memory_space=pltpu.VMEM)
-    sends = 3 * (n_exp - 1) + GATHER_SENDS + 4 + 2 + 4
+    sends = (2 + CHUNKS) * (n_exp - 1) + GATHER_SENDS + 4 + 2 + 4
     return pl.pallas_call(
         functools.partial(expert_kernel, n_exp),
         out_shape=jax.ShapeDtypeStruct((tokens, width), bf16),
-        in_specs=[vmem] * 5 + [pl.BlockSpec(memory_space=pl.ANY)] * 3,
+        in_specs=[vmem] * 5 + [pl.BlockSpec(memory_space=pl.ANY)] * 4,
         out_specs=vmem,
         scratch_shapes=[
+            pltpu.VMEM(out_proj.shape, bf16),
+            pltpu.VMEM((gated.shape[0], width), bf16),
+            pltpu.VMEM((tokens, width), bf16),
             pltpu.VMEM(gate_proj.shape[1:], bf16),
             pltpu.VMEM(up_proj.shape[1:], bf16),
             pltpu.VMEM(down_proj.shape[1:], bf16),
             pltpu.VMEM((n_exp - 1, tokens, width), bf16),
             pltpu.VMEM((n_exp, cap, width), bf16),
             pltpu.VMEM((8, rows, width), bf16),
-            pltpu.VMEM((4 * rows, gate_proj.shape[2]), bf16),
+            pltpu.VMEM((8 * rows, gate_proj.shape[2]), bf16),
             pltpu.VMEM((8, rows, width), bf16),
             pltpu.VMEM((4, rows, width), bf16),
             pltpu.VMEM((2, rows // 2, width), bf16),
             pltpu.VMEM((2, rows, width), bf16),
             pltpu.VMEM((rows, width), bf16),
             pltpu.VMEM((n_exp, cap, width), bf16),
+            dma((CHUNKS,)),
             dma((3,)),
             dma((sends,)),
-            dma((n_exp - 1,)),
+            dma((n_exp - 1, CHUNKS)),
             dma((n_exp - 1,)),
             dma((8, 2)),
             dma((4,)),
@@ -391,11 +431,12 @@
             transcendentals=0,
         ),
     )(
-        partial_out,
+        gated,
         residual,
         norm_gain.reshape(1, width),
         select,
         combine,
+        out_proj,
         gate_proj,
         up_proj,
         down_proj,
@@ -514,7 +555,6 @@
         correction = correction + output_c[state_index][:, None] * weight_row
     mixer_y = local_y + correction + skip_gain * x_float
     gated = (mixer_y * jax.nn.silu(mixer_z.astype(jnp.float32))).astype(jnp.bfloat16)
-    partial_out = jnp.dot(gated, out_proj, preferred_element_type=jnp.float32)
     slot_count = experts_all * capacity
     per_device = experts_local * capacity
     target_index = jnp.where(slot_ids >= 0, expert_ids * capacity + slot_ids, -1)
@@ -529,17 +569,19 @@
     )
     if cube:
         return fast_experts(
-            partial_out.astype(jnp.bfloat16),
+            gated,
             residual,
             norm_gain,
             select,
             combine,
+            out_proj,
             gate_proj,
             up_proj,
             down_proj,
             n_exp,
             capacity,
         )
+    partial_out = jnp.dot(gated, out_proj, preferred_element_type=jnp.float32)
     summed = lax.psum(partial_out.astype(jnp.bfloat16), "exp").astype(jnp.float32)
     mixer_out = lax.dynamic_slice_in_dim(summed, lax.axis_index("exp") * tok_dev, tok_dev, 0)
     hidden_one = (residual.astype(jnp.float32) + mixer_out).astype(jnp.bfloat16)

time: 105 us -> 102 us (0.971)
  matrix products: 4.9 us -> 0 us
  other arithmetic: 11.5 us -> 13.5 us
    dot_general x1 -> x0, matrix products: 4.9 us -> none  [on_device(): partial_out = jnp.dot(gated, out_proj, preferred_element_type=jnp.float32)]
    convert_element_type x0 -> x1, other arithmetic: none -> 1.94 us  [on_device(): (mixer_y * jax.nn.silu(mixer_z.astype(jnp.float32))).astype(jnp.bfloat16)]
where the time goes in v2:
time: 102 us; the launch traced here: 101 us
  Pallas kernels  75.5 us (74%)
  other arithmetic  13.5 us (13%)
  local copies, waits for them, and re-layouts  10.2 us (10%)
  loops' own time  1.66 us (2%)
    pallas_call x1, Pallas kernels, fast_experts(): pl.pallas_call(functools.partial(expert_kernel, n_exp), out_shape=jax.Sha...  63.8 us
    pallas_call x1, Pallas kernels, fast_prefix(): pl.pallas_call(prefix_kernel, out_shape=jax.ShapeDtypeStruct(final_state....  11.7 us
    reduce_sum x48, other arithmetic, advance(): outputs.append(jnp.sum(c_blk[inner_pos][:, None] * state, axis=0))  6.82 us
    unnamed x23, local copies, waits for them, and re-layouts  2.9 us

profile of v2, /device:TPU:0, one launch (start us, length us, event | category | flops | bytes accessed | tf_op | source)
XLA Modules:
  0.0 101.1 jit_solution(13235877809225051985)
XLA Ops:
  0.0 0.9 exponential_negate_fusion
  0.9 1.0 convert_bitcast_fusion
  1.9 1.3 %fusion.7 = f32[16,8,1024]{2,1,0:T(8,128)S(1)} fusion(f32[128,1024]{1,0:T(8,128)} %param.20), kind=kLoop, calls=%fused_computation.65 | loop fusion | flops 786432 | bytes 1048576 | tf_op jit(solution)/shard_map/reshape | solution.py:478
  3.2 0.8 copy.25
  4.0 0.8 copy.26
  4.9 13.4 %while.17 = (s32[]{:T(128)}, f32[16,1024]{1,0:T(8,128)S(1)}, f32[1024]{0:T(1024)S(1)}, f32[16,8,1024]{2,1,0:T(8,128)S(1)}, f32[16,8,1024]{2,1,0:T(8,128)S(1)}, /...) while((s32[]{:T(128)}, f32[16,1024]{1,0:T(8,128)S(1)}, ...), condition=%wide.region_9.10_spmd.clone, body=%wide.region_0.9_spmd.clone.sunk | while | flops 1156106 | bytes 1459865 | solution.py:500
  5.1 0.2 multiply_reduce_fusion.11
  5.3 0.1 multiply_reduce_fusion.13
  5.4 0.1 multiply_reduce_fusion.12
  5.9 0.2 multiply_reduce_fusion.11
  6.1 0.1 multiply_reduce_fusion.13
  6.3 0.1 multiply_reduce_fusion.12
  6.8 0.2 multiply_reduce_fusion.11
  7.0 0.1 multiply_reduce_fusion.13
  7.1 0.1 multiply_reduce_fusion.12
  7.6 0.2 multiply_reduce_fusion.11
  7.8 0.1 multiply_reduce_fusion.13
  7.9 0.1 multiply_reduce_fusion.12
  8.5 0.2 multiply_reduce_fusion.11
  8.6 0.1 multiply_reduce_fusion.13
  8.8 0.1 multiply_reduce_fusion.12
  9.3 0.2 multiply_reduce_fusion.11
  9.5 0.1 multiply_reduce_fusion.13
  9.6 0.1 multiply_reduce_fusion.12
  10.1 0.2 multiply_reduce_fusion.11
  10.3 0.1 multiply_reduce_fusion.13
  10.5 0.1 multiply_reduce_fusion.12
  11.0 0.2 multiply_reduce_fusion.11
  11.2 0.1 multiply_reduce_fusion.13
  11.3 0.1 multiply_reduce_fusion.12
  11.8 0.2 multiply_reduce_fusion.11
  12.0 0.1 multiply_reduce_fusion.13
  12.1 0.1 multiply_reduce_fusion.12
  12.7 0.2 multiply_reduce_fusion.11
  12.8 0.1 multiply_reduce_fusion.13
  13.0 0.1 multiply_reduce_fusion.12
  13.5 0.2 multiply_reduce_fusion.11
  13.7 0.1 multiply_reduce_fusion.13
  13.8 0.1 multiply_reduce_fusion.12
  14.3 0.2 multiply_reduce_fusion.11
  14.5 0.1 multiply_reduce_fusion.13
  14.7 0.1 multiply_reduce_fusion.12
  15.2 0.2 multiply_reduce_fusion.11
  15.3 0.1 multiply_reduce_fusion.13
  15.5 0.1 multiply_reduce_fusion.12
  16.0 0.2 multiply_reduce_fusion.11
  16.2 0.1 multiply_reduce_fusion.13
  16.3 0.1 multiply_reduce_fusion.12
  16.9 0.2 multiply_reduce_fusion.11
  17.0 0.1 multiply_reduce_fusion.13
  17.2 0.1 multiply_reduce_fusion.12
  17.7 0.2 multiply_reduce_fusion.11
  17.9 0.1 multiply_reduce_fusion.13
  18.0 0.1 multiply_reduce_fusion.12
  18.4 0.6 pad_maximum_fusion.local_ref
  19.1 11.7 %shard_map.154 = f32[16,1024]{1,0:T(8,128)} custom-call(bf16[32,1024]{1,0:T(8,128)(2,1)} %pad_maximum_fusion.local_ref), custom_call_target="tpu_custom_call" | custom-call | flops 1000000 | bytes 1000000 | tf_op jit(solution)/shard_map/pallas_call | solution.py:142
  30.8 1.3 %fusion.75 = (f32[1,1024]{1,0:T(1,128)S(1)}, f32[1,1024]{1,0:T(1,128)S(1)}, f32[1,1024]{1,0:T(1,128)S(1)}, f32[1,1024]{1,0:T(1,128)S(1)}, f32[1,1024]{1,0:T(1,12...) fusion(f32[16,1024]{1,0:T(8,128)} %shard_map.154), kind=kLoop, calls=%fused_computation.172 | loop fusion | bytes 131072 | tf_op jit(solution)/shard_map/slice | solution.py:553
  32.2 1.9 %fusion.3.gated_ref = bf16[128,1024]{1,0:T(8,128)(2,1)S(1)} fusion(bf16[128,1024]{1,0:T(8,128)(2,1)S(1)} %copy-done.3, bf16[128,1024]{1,0:T(8,128)(2,1)S(1)} %copy-done.9, f32[16,8,1024]{2,1,0:T(8,128)S(1)} %get-tuple-element.61, f32[16,8,1024]{2,1,0:T(8,128)S(1)} %get-tuple-element.60, f32[1024]{0:T(1024)S(1)} %copy-done.10, f32[1024]{0:T(1024)S(1)} %bitcast.441, ...), kind=kLoop, calls=%fused_computation.61 | loop fusion | flops 9699328 | bytes 1978368 | tf_op jit(solution)/shard_map/convert_element_type | solution.py:557
  34.2 0.1 fusion.72
  34.3 0.1 copy.27.select_ref
  34.4 0.1 select_reduce_fusion.combine_ref
  34.5 2.2 %copy-done = bf16[1024,2048]{1,0:T(8,128)(2,1)S(1)} copy-done((bf16[1024,2048]{1,0:T(8,128)(2,1)S(1)}, bf16[1024,2048]{1,0:T(8,128)(2,1)}, u32[]{:S(2)}) %copy-start) | copy-done | bytes 4194328
  36.7 63.8 %shard_map.155 = bf16[32,2048]{1,0:T(8,128)(2,1)S(1)} custom-call(bf16[128,1024]{1,0:T(8,128)(2,1)S(1)} %fusion.3.gated_ref, bf16[32,2048]{1,0:T(8,128)(2,1)S(1)} %copy-done.1, f32[1,2048]{1,0:T(1,128)S(1)} %bitcast.390, bf16[64,32]{1,0:T(8,128)(2,1)S(1)} %copy.27.select_ref, f32[32,64]{1,0:T(8,128)S(1)} %select_reduce_fusion.combine_ref, ...), custom_call_target="tpu_custom_call" | custom-call | flops 6442450944 | bytes 12582912 | tf_op jit(solution)/shard_map/pallas_call | solution.py:392
  100.4 0.7 copy.46
  (207 shorter events, 5.1 us)
Async XLA Ops:
  4.8 13.6 %copy-start.4 = (f32[16,1024]{1,0:T(8,128)S(1)}, f32[16,1024]{1,0:T(8,128)}, u32[]{:S(2)}) copy-start(f32[16,1024]{1,0:T(8,128)} %param.23) | copy-start | bytes 196612
  4.8 27.3 %copy-start.5 = (f32[16,128]{1,0:T(8,128)S(1)}, f32[16,128]{1,0:T(8,128)}, u32[]{:S(2)}) copy-start(f32[16,128]{1,0:T(8,128)} %param.22) | copy-start | bytes 24580
  4.8 27.3 %copy-start.3 = (bf16[128,1024]{1,0:T(8,128)(2,1)S(1)}, bf16[128,1024]{1,0:T(8,128)(2,1)}, u32[]{:S(2)}) copy-start(bf16[128,1024]{1,0:T(8,128)(2,1)} %param.18) | copy-start | bytes 786436
  4.8 27.3 %copy-start.9 = (bf16[128,1024]{1,0:T(8,128)(2,1)S(1)}, bf16[128,1024]{1,0:T(8,128)(2,1)}, u32[]{:S(2)}) copy-start(bf16[128,1024]{1,0:T(8,128)(2,1)} %param.19) | copy-start | bytes 786436
  4.9 27.3 %copy-start.10 = (f32[1024]{0:T(1024)S(1)}, f32[1024]{0:T(1024)}, u32[]{:S(2)}) copy-start(f32[1024]{0:T(1024)} %param.24) | copy-start | bytes 12292
  18.3 15.8 %copy-start.6 = (s32[32,2]{0,1:T(2,128)S(1)}, s32[32,2]{0,1:T(2,128)}, u32[]{:S(2)}) copy-start(s32[32,2]{0,1:T(2,128)} %param.32) | copy-start | bytes 772
  18.3 15.8 %copy-start.7 = (s32[32,2]{0,1:T(2,128)S(1)}, s32[32,2]{0,1:T(2,128)}, u32[]{:S(2)}) copy-start(s32[32,2]{0,1:T(2,128)} %param.31) | copy-start | bytes 772
  18.3 16.0 %copy-start.8 = (f32[32,2]{0,1:T(2,128)S(1)}, f32[32,2]{0,1:T(2,128)}, u32[]{:S(2)}) copy-start(f32[32,2]{0,1:T(2,128)} %param.33) | copy-start | bytes 772
  18.3 16.1 %copy-start.1 = (bf16[32,2048]{1,0:T(8,128)(2,1)S(1)}, bf16[32,2048]{1,0:T(8,128)(2,1)}, u32[]{:S(2)}) copy-start(bf16[32,2048]{1,0:T(8,128)(2,1)} %residual_ref.1) | copy-start | bytes 393220
  18.4 16.1 %copy-start.2 = (f32[2048]{0:T(1024)S(1)}, f32[2048]{0:T(1024)}, u32[]{:S(2)}) copy-start(f32[2048]{0:T(1024)} %param.27) | copy-start | bytes 24580
  34.5 2.2 %copy-start = (bf16[1024,2048]{1,0:T(8,128)(2,1)S(1)}, bf16[1024,2048]{1,0:T(8,128)(2,1)}, u32[]{:S(2)}) copy-start(bf16[1024,2048]{1,0:T(8,128)(2,1)} %proj_hbm.1) | copy-start | bytes 12582916

commit v3 on v2

--- a/solution.py
+++ b/solution.py
@@ -112,23 +112,72 @@
 
 
 GATHER_SENDS = 14
+LOG2_E = 1.4426950408889634
 CHUNKS = 4
 
 
-def prefix_kernel(local_ref, carried_ref, slots, send_sem, sems):
+def mixer_kernel(
+    raw_ref,
+    x_ref,
+    b_ref,
+    c_ref,
+    log_ref,
+    y_ref,
+    cumulative_ref,
+    carried_ref,
+    step_ref,
+    slots,
+    send_sem,
+    sems,
+):
     links = Links(send_sem)
     greet(links, 1)
-    slots[0] = local_ref[...]
+    tokens, width = raw_ref.shape
+    states, lanes = b_ref.shape[1:]
+    decay_two = jnp.exp(log_ref[...]) * (-LOG2_E)
+
+    def over_width(value):
+        return jnp.concatenate([value] * (width // lanes), axis=1)
+
+    def advance(j, state):
+        rows = pl.ds(pl.multiple_of(j * 8, 8), 8)
+        raw = raw_ref[rows, :]
+        step = jnp.maximum(raw, 0.0) + jnp.log1p(jnp.exp(-jnp.abs(raw)))
+        step_ref[rows, :] = step
+        scaled = step * x_ref[rows, :].astype(jnp.float32)
+        outputs = []
+        for i in range(8):
+            here = b_ref[j * 8 + i]
+            seen = c_ref[j * 8 + i]
+            state = jnp.exp2(step[i : i + 1] * decay_two) * state + scaled[
+                i : i + 1
+            ] * over_width(here)
+            outputs.append(jnp.sum(over_width(seen) * state, axis=0, keepdims=True))
+        y_ref[rows, :] = jnp.concatenate(outputs, axis=0)
+        return state
+
+    start = jnp.zeros((states, width), jnp.float32)
+    final_state = lax.fori_loop(0, tokens // 8, advance, start)
+    total_step = jnp.sum(step_ref[...], axis=0, keepdims=True)
+    slots[0, 0:states] = jnp.exp2(total_step * decay_two).astype(jnp.bfloat16)
+    slots[0, states : 2 * states] = final_state.astype(jnp.bfloat16)
     gather = Gather(links, slots, sems)
     gather.begin(0)
     gather.begin(1)
+    row = lax.broadcasted_iota(jnp.int32, (tokens, tokens), 0)
+    column = lax.broadcasted_iota(jnp.int32, (tokens, tokens), 1)
     gather.forward_near()
     gather.forward_far()
+    cumulative_ref[...] = jnp.dot(
+        (column <= row).astype(jnp.float32),
+        step_ref[...],
+        precision=lax.Precision.HIGHEST,
+        preferred_element_type=jnp.float32,
+    )
     for mask in (1, 3, 5, 7):
         gather.wait(mask, 0)
         gather.wait(mask, 1)
-    states = carried_ref.shape[0]
-    state = jnp.zeros_like(carried_ref)
+    state = start
     for k in range(7):
         block = slots[links.ctx ^ k].astype(jnp.float32)
         after = block[:states] * state + block[states:]
@@ -137,28 +186,43 @@
     links.finish()
 
 
-def fast_prefix(through_final, final_state):
-    local = jnp.concatenate([through_final, final_state], axis=0).astype(jnp.bfloat16)
+def fast_mixer(step_raw, mixer_x, input_b, output_c, decay_log):
+    tokens, width = step_raw.shape
+    states = input_b.shape[0]
+    lanes = 128
+
+    def spread(value):
+        return jnp.broadcast_to(value.T[:, :, None], (tokens, states, lanes))
+
+    vmem = pl.BlockSpec(memory_space=pltpu.VMEM)
+    full = jax.ShapeDtypeStruct((tokens, width), jnp.float32)
     return pl.pallas_call(
-        prefix_kernel,
-        out_shape=jax.ShapeDtypeStruct(final_state.shape, jnp.float32),
-        in_specs=[pl.BlockSpec(memory_space=pltpu.VMEM)],
-        out_specs=pl.BlockSpec(memory_space=pltpu.VMEM),
+        mixer_kernel,
+        out_shape=(full, full, jax.ShapeDtypeStruct((states, width), jnp.float32)),
+        in_specs=[vmem] * 5,
+        out_specs=(vmem, vmem, vmem),
         scratch_shapes=[
-            pltpu.VMEM((8,) + local.shape, jnp.bfloat16),
+            pltpu.VMEM((tokens, width), jnp.float32),
+            pltpu.VMEM((8, 2 * states, width), jnp.bfloat16),
             pltpu.SemaphoreType.DMA((GATHER_SENDS,)),
             pltpu.SemaphoreType.DMA((8, 2)),
         ],
-        compiler_params=pltpu.CompilerParams(collective_id=1, has_side_effects=True),
-        cost_estimate=pl.CostEstimate(flops=10**6, bytes_accessed=10**6, transcendentals=0),
-    )(local)
+        compiler_params=pltpu.CompilerParams(
+            collective_id=1, has_side_effects=True, vmem_limit_bytes=24 * 1024 * 1024
+        ),
+        cost_estimate=pl.CostEstimate(
+            flops=8 * tokens * states * width,
+            bytes_accessed=16 * tokens * width,
+            transcendentals=tokens * states * width,
+        ),
+    )(step_raw, mixer_x, spread(input_b), spread(output_c), decay_log)
 
 
 def expert_kernel(
     n_exp,
     gated_ref,
-    residual_ref,
-    gain_ref,
+    residual_hbm,
+    gain_hbm,
     select_ref,
     combine_ref,
     proj_hbm,
@@ -166,6 +230,8 @@
     up_hbm,
     down_hbm,
     out_ref,
+    residual_ref,
+    gain_ref,
     proj_ref,
     partial,
     hidden_one,
@@ -194,7 +260,7 @@
     return_sem,
 ):
     links = Links(send_sem)
-    tokens = residual_ref.shape[0]
+    tokens = hidden_one.shape[0]
     cap = dispatch.shape[1]
     half_rows = total.shape[0] // 2
     halves = (pl.ds(0, half_rows), pl.ds(half_rows, half_rows))
@@ -211,7 +277,11 @@
             ((gate_hbm, gate_ref), (up_hbm, up_ref), (down_hbm, down_ref))
         )
     ]
-    for load in proj_loads + loads:
+    row_loads = [
+        pltpu.make_async_copy(residual_hbm, residual_ref, load_sem.at[3]),
+        pltpu.make_async_copy(gain_hbm, gain_ref, load_sem.at[4]),
+    ]
+    for load in proj_loads + row_loads + loads:
         load.start()
     greet(links, n_exp)
 
@@ -230,6 +300,8 @@
                 sum_sem.at[gap - 1, k],
                 peer,
             )
+    for load in row_loads:
+        load.wait()
     for k, columns in enumerate(column_chunks):
         mixer_out = partial[token_rows(exp), columns].astype(jnp.float32)
         for gap in range(1, n_exp):
@@ -388,13 +460,16 @@
     bf16 = jnp.bfloat16
     dma = pltpu.SemaphoreType.DMA
     vmem = pl.BlockSpec(memory_space=pltpu.VMEM)
+    hbm = pl.BlockSpec(memory_space=pl.ANY)
     sends = (2 + CHUNKS) * (n_exp - 1) + GATHER_SENDS + 4 + 2 + 4
     return pl.pallas_call(
         functools.partial(expert_kernel, n_exp),
         out_shape=jax.ShapeDtypeStruct((tokens, width), bf16),
-        in_specs=[vmem] * 5 + [pl.BlockSpec(memory_space=pl.ANY)] * 4,
+        in_specs=[vmem] + [hbm] * 2 + [vmem] * 2 + [hbm] * 4,
         out_specs=vmem,
         scratch_shapes=[
+            pltpu.VMEM((tokens, width), bf16),
+            pltpu.VMEM((1, width), jnp.float32),
             pltpu.VMEM(out_proj.shape, bf16),
             pltpu.VMEM((gated.shape[0], width), bf16),
             pltpu.VMEM((tokens, width), bf16),
@@ -412,7 +487,7 @@
             pltpu.VMEM((rows, width), bf16),
             pltpu.VMEM((n_exp, cap, width), bf16),
             dma((CHUNKS,)),
-            dma((3,)),
+            dma((5,)),
             dma((sends,)),
             dma((n_exp - 1, CHUNKS)),
             dma((n_exp - 1,)),
@@ -522,14 +597,8 @@
     route_weight,
 ):
     n_exp = lax.axis_size("exp")
-    step_size = jax.nn.softplus(step_raw)
     decay_rate = -jnp.exp(decay_log)
     x_float = mixer_x.astype(jnp.float32)
-    final_state, total_step, local_y, cumulative = local_recurrence(
-        step_size, x_float, input_b, output_c, decay_rate
-    )
-    through_final = jnp.exp(total_step[None, :] * decay_rate)
-    identity = (jnp.ones_like(through_final), jnp.zeros_like(final_state))
     tok_dev = residual.shape[0]
     model_width = residual.shape[1]
     experts_local = gate_proj.shape[0]
@@ -542,9 +611,30 @@
         and capacity % 16 == 0
         and tok_dev % 16 == 0
     )
+    slot_count = experts_all * capacity
+    per_device = experts_local * capacity
+    target_index = jnp.where(slot_ids >= 0, expert_ids * capacity + slot_ids, -1)
+    slot_iota = jnp.arange(slot_count, dtype=jnp.int32)
+    select = jnp.any(target_index[None, :, :] == slot_iota[:, None, None], axis=-1).astype(
+        jnp.bfloat16
+    )
+    matches = target_index[:, :, None] == slot_iota[None, None, :]
+    combine = jnp.sum(
+        jnp.where(matches, route_weight[:, :, None], jnp.zeros_like(route_weight)[:, :, None]),
+        axis=1,
+    )
     if cube:
-        carried_state = fast_prefix(through_final, final_state)
+        step_raw, select, combine = lax.optimization_barrier((step_raw, select, combine))
+        local_y, cumulative, carried_state = fast_mixer(
+            step_raw, mixer_x, input_b, output_c, decay_log
+        )
     else:
+        step_size = jax.nn.softplus(step_raw)
+        final_state, total_step, local_y, cumulative = local_recurrence(
+            step_size, x_float, input_b, output_c, decay_rate
+        )
+        through_final = jnp.exp(total_step[None, :] * decay_rate)
+        identity = (jnp.ones_like(through_final), jnp.zeros_like(final_state))
         carried_state = prefix((through_final, final_state), "ctx", link_states, identity)[1]
     correction = jnp.zeros_like(local_y)
     for state_index in range(decay_rate.shape[0]):
@@ -555,18 +645,6 @@
         correction = correction + output_c[state_index][:, None] * weight_row
     mixer_y = local_y + correction + skip_gain * x_float
     gated = (mixer_y * jax.nn.silu(mixer_z.astype(jnp.float32))).astype(jnp.bfloat16)
-    slot_count = experts_all * capacity
-    per_device = experts_local * capacity
-    target_index = jnp.where(slot_ids >= 0, expert_ids * capacity + slot_ids, -1)
-    slot_iota = jnp.arange(slot_count, dtype=jnp.int32)
-    select = jnp.any(target_index[None, :, :] == slot_iota[:, None, None], axis=-1).astype(
-        jnp.bfloat16
-    )
-    matches = target_index[:, :, None] == slot_iota[None, None, :]
-    combine = jnp.sum(
-        jnp.where(matches, route_weight[:, :, None], jnp.zeros_like(route_weight)[:, :, None]),
-        axis=1,
-    )
     if cube:
         return fast_experts(
             gated,

time: 102 us -> 88 us (0.86)
  other arithmetic: 13.5 us -> 3.56 us
  local copies, waits for them, and re-layouts: 10.2 us -> 5.98 us
  Pallas kernels: 75.5 us -> 77.9 us
  loops' own time: 1.66 us -> 0 us
    reduce_sum x48 -> x0, other arithmetic: 6.82 us -> none  [advance(): outputs.append(jnp.sum(c_blk[inner_pos][:, None] * state, axis=0))]
    pallas_call x1, Pallas kernels: 11.7 us -> 14.1 us  [fast_mixer(): pl.pallas_call(mixer_kernel, out_shape=(full, full, jax.ShapeDtypeStruct(...]
    reshape x2 -> x0, other arithmetic: 2.31 us -> none  [the longest x1 1.32 us: local_recurrence(): step_blocks = step_size.reshape(16, sub_len, width)]
    another operation x32 -> x0, local copies, waits for them, and re-layouts: 2.04 us -> none  [advance(): return ((state, run_step), (jnp.stack(outputs), jnp.stack(totals)))]
    another operation x1 -> x0, loops' own time: 1.66 us -> none  [local_recurrence(): lax.scan(advance, start, (step_blocks, x_blocks, b_blocks, c_blocks))]
    slice x32 -> x0, local copies, waits for them, and re-layouts: 1.34 us -> none  [the longest x16 0.69 us: advance(): x_blk[inner_pos]]
    slice x1, local copies, waits for them, and re-layouts: 1.3 us -> 0.05 us  [on_device(): carried_state[state_index][None, :]]
    unnamed x23 -> x19, local copies, waits for them, and re-layouts: 2.9 us -> 3.51 us
where the time goes in v3:
time: 88 us; the launch traced here: 87.6 us
  Pallas kernels  77.9 us (89%)
  local copies, waits for them, and re-layouts  5.98 us (7%)
  other arithmetic  3.56 us (4%)
    pallas_call x1, Pallas kernels, fast_experts(): pl.pallas_call(functools.partial(expert_kernel, n_exp), out_shape=jax.Sha...  63.9 us
    pallas_call x1, Pallas kernels, fast_mixer(): pl.pallas_call(mixer_kernel, out_shape=(full, full, jax.ShapeDtypeStruct(...  14.1 us
    unnamed x19, local copies, waits for them, and re-layouts  3.51 us
    convert_element_type x1, other arithmetic, on_device(): (mixer_y * jax.nn.silu(mixer_z.astype(jnp.float32))).astype(jnp.bfloat16)  1.95 us

profile of v3, /device:TPU:0, one launch (start us, length us, event | category | flops | bytes accessed | tf_op | source)
XLA Modules:
  0.0 87.6 jit_solution(3675568116246475214)
XLA Ops:
  0.0 0.0 copy-start.6
  0.0 0.0 copy-start.7
  0.0 0.0 copy-start.8
  0.0 0.7 compare_select_fusion
  0.8 0.1 fusion.5
  0.8 0.1 copy.22
  0.9 0.8 select_reduce_fusion.combine_ref
  1.7 0.8 copy.23
  2.5 0.3 broadcast_in_dim.27.b_ref
  2.9 0.8 copy.24
  3.7 0.3 broadcast_in_dim.42.c_ref
  4.0 0.0 copy-start
  4.0 0.8 copy-done
  4.8 0.0 copy-start.2
  4.8 1.0 %copy-done.2 = f32[128,1024]{1,0:T(8,128)S(1)} copy-done((f32[128,1024]{1,0:T(8,128)S(1)}, f32[128,1024]{1,0:T(8,128)}, u32[]{:S(2)}) %copy-start.2) | copy-done | bytes 524312
  5.9 0.0 copy-start.3
  5.9 0.9 %copy-done.3 = bf16[128,1024]{1,0:T(8,128)(2,1)S(1)} copy-done((bf16[128,1024]{1,0:T(8,128)(2,1)S(1)}, bf16[128,1024]{1,0:T(8,128)(2,1)}, u32[]{:S(2)}) %copy-start.3) | copy-done | bytes 262168
  6.8 0.0 copy-start.1
  6.8 0.0 copy-start.4
  6.8 0.0 copy-start.5
  6.8 14.1 %shard_map.154 = (f32[128,1024]{1,0:T(8,128)S(1)}, f32[128,1024]{1,0:T(8,128)S(1)}, f32[16,1024]{1,0:T(8,128)S(1)}) custom-call(f32[128,1024]{1,0:T(8,128)S(1)} %copy-done.2, bf16[128,1024]{1,0:T(8,128)(2,1)S(1)} %copy-done.3, f32[128,16,128]{2,1,0:T(8,128)S(1)} %broadcast_in_dim.27.b_ref, f32[128,16,128]{2,1,0:T(8,128)S(1)} %broadcast_in_dim.42.c_ref, ...), custom_call_target="tpu_custom_call" | custom-call | flops 16777216 | bytes 2097152 | tf_op jit(solution)/shard_map/pallas_call | solution.py:199
  21.1 0.0 copy-done.6
  21.1 0.0 copy-done.7
  21.1 0.0 copy-done.8
  21.1 2.0 %fusion.4.gated_ref = bf16[128,1024]{1,0:T(8,128)(2,1)S(1)} fusion(bf16[128,1024]{1,0:T(8,128)(2,1)S(1)} %copy-done.7, bf16[128,1024]{1,0:T(8,128)(2,1)S(1)} %copy-done.3, f32[128,1024]{1,0:T(8,128)S(1)} %get-tuple-element.12, f32[128,1024]{1,0:T(8,128)S(1)} %get-tuple-element.13, f32[1024]{0:T(1024)S(1)} %copy-done.8, f32[1024]{0:T(1024)S(1)} %bitcast.71, ...), kind=kLoop, calls=%fused_computation.6 | loop fusion | flops 9699328 | bytes 1978368 | tf_op jit(solution)/shard_map/convert_element_type | solution.py:647
  23.1 0.0 copy-done.1
  23.1 0.0 copy-done.4
  23.1 0.0 copy-done.5
  23.1 63.9 %shard_map.155 = bf16[32,2048]{1,0:T(8,128)(2,1)S(1)} custom-call(bf16[128,1024]{1,0:T(8,128)(2,1)S(1)} %fusion.4.gated_ref, bf16[32,2048]{1,0:T(8,128)(2,1)S(1)} %copy-done.4, f32[1,2048]{1,0:T(1,128)S(1)} %bitcast.67, bf16[64,32]{1,0:T(8,128)(2,1)S(1)} %convert_element_type.12.select_ref, f32[32,64]{1,0:T(8,128)S(1)} %select_reduce_fusion.combine_ref, ...), custom_call_target="tpu_custom_call" | custom-call | flops 6442450944 | bytes 12582912 | tf_op jit(solution)/shard_map/pallas_call | solution.py:465
  87.0 0.7 copy.26
  (5 shorter events, 0.1 us)
Async XLA Ops:
  0.0 21.1 %copy-start.6 = (f32[16,128]{1,0:T(8,128)S(1)}, f32[16,128]{1,0:T(8,128)}, u32[]{:S(2)}) copy-start(f32[16,128]{1,0:T(8,128)} %param.20) | copy-start | bytes 24580
  0.0 21.1 %copy-start.7 = (bf16[128,1024]{1,0:T(8,128)(2,1)S(1)}, bf16[128,1024]{1,0:T(8,128)(2,1)}, u32[]{:S(2)}) copy-start(bf16[128,1024]{1,0:T(8,128)(2,1)} %param.17) | copy-start | bytes 786436
  0.0 21.1 %copy-start.8 = (f32[1024]{0:T(1024)S(1)}, f32[1024]{0:T(1024)}, u32[]{:S(2)}) copy-start(f32[1024]{0:T(1024)} %param.22) | copy-start | bytes 12292
  4.0 0.8 copy-start
  4.8 1.0 %copy-start.2 = (f32[128,1024]{1,0:T(8,128)S(1)}, f32[128,1024]{1,0:T(8,128)}, u32[]{:S(2)}) copy-start(f32[128,1024]{1,0:T(8,128)} %raw_ref) | copy-start | bytes 1572868
  5.9 0.9 %copy-start.3 = (bf16[128,1024]{1,0:T(8,128)(2,1)S(1)}, bf16[128,1024]{1,0:T(8,128)(2,1)}, u32[]{:S(2)}) copy-start(bf16[128,1024]{1,0:T(8,128)(2,1)} %x_ref.1) | copy-start | bytes 786436
  6.8 16.2 %copy-start.1 = (bf16[1024,2048]{1,0:T(8,128)(2,1)S(1)}, bf16[1024,2048]{1,0:T(8,128)(2,1)}, u32[]{:S(2)}) copy-start(bf16[1024,2048]{1,0:T(8,128)(2,1)} %proj_hbm.1) | copy-start | bytes 12582916
  6.8 16.3 %copy-start.4 = (bf16[32,2048]{1,0:T(8,128)(2,1)S(1)}, bf16[32,2048]{1,0:T(8,128)(2,1)}, u32[]{:S(2)}) copy-start(bf16[32,2048]{1,0:T(8,128)(2,1)} %residual_hbm.1) | copy-start | bytes 393220
  6.8 16.3 %copy-start.5 = (f32[2048]{0:T(1024)S(1)}, f32[2048]{0:T(1024)}, u32[]{:S(2)}) copy-start(f32[2048]{0:T(1024)} %param.25) | copy-start | bytes 24580

commit v4 on v3

--- a/solution.py
+++ b/solution.py
@@ -624,7 +624,7 @@
         axis=1,
     )
     if cube:
-        step_raw, select, combine = lax.optimization_barrier((step_raw, select, combine))
+        decay_log, select, combine = lax.optimization_barrier((decay_log, select, combine))
         local_y, cumulative, carried_state = fast_mixer(
             step_raw, mixer_x, input_b, output_c, decay_log
         )

time: 88 us -> 88 us (level)
  no operation moved by 1% of the time
where the time goes in v4:
time: 88 us; the launch traced here: 87.6 us
  Pallas kernels  77.9 us (89%)
  local copies, waits for them, and re-layouts  5.98 us (7%)
  other arithmetic  3.56 us (4%)
    pallas_call x1, Pallas kernels, fast_experts(): pl.pallas_call(functools.partial(expert_kernel, n_exp), out_shape=jax.Sha...  63.9 us
    pallas_call x1, Pallas kernels, fast_mixer(): pl.pallas_call(mixer_kernel, out_shape=(full, full, jax.ShapeDtypeStruct(...  14.1 us
    unnamed x19, local copies, waits for them, and re-layouts  3.51 us
    convert_element_type x1, other arithmetic, on_device(): (mixer_y * jax.nn.silu(mixer_z.astype(jnp.float32))).astype(jnp.bfloat16)  1.95 us

profile of v4, /device:TPU:0, one launch (start us, length us, event | category | flops | bytes accessed | tf_op | source)
XLA Modules:
  0.0 87.6 jit_solution(3675568116246475214)
XLA Ops:
  0.0 0.0 copy-start.6
  0.0 0.0 copy-start.7
  0.0 0.0 copy-start.8
  0.0 0.7 compare_select_fusion
  0.8 0.1 fusion.5
  0.8 0.1 copy.24
  0.9 0.8 select_reduce_fusion.combine_ref
  1.7 0.8 copy.22
  2.5 0.3 broadcast_in_dim.24.b_ref
  2.9 0.8 copy.23
  3.7 0.3 broadcast_in_dim.25.c_ref
  4.0 0.0 copy-start
  4.0 0.8 copy-done
  4.8 0.0 copy-start.2
  4.8 1.0 %copy-done.2 = f32[128,1024]{1,0:T(8,128)S(1)} copy-done((f32[128,1024]{1,0:T(8,128)S(1)}, f32[128,1024]{1,0:T(8,128)}, u32[]{:S(2)}) %copy-start.2) | copy-done | bytes 524312
  5.9 0.0 copy-start.3
  5.9 0.9 %copy-done.3 = bf16[128,1024]{1,0:T(8,128)(2,1)S(1)} copy-done((bf16[128,1024]{1,0:T(8,128)(2,1)S(1)}, bf16[128,1024]{1,0:T(8,128)(2,1)}, u32[]{:S(2)}) %copy-start.3) | copy-done | bytes 262168
  6.8 0.0 copy-start.1
  6.8 0.0 copy-start.4
  6.8 0.0 copy-start.5
  6.8 14.1 %shard_map.154 = (f32[128,1024]{1,0:T(8,128)S(1)}, f32[128,1024]{1,0:T(8,128)S(1)}, f32[16,1024]{1,0:T(8,128)S(1)}) custom-call(f32[128,1024]{1,0:T(8,128)S(1)} %copy-done.2, bf16[128,1024]{1,0:T(8,128)(2,1)S(1)} %copy-done.3, f32[128,16,128]{2,1,0:T(8,128)S(1)} %broadcast_in_dim.24.b_ref, f32[128,16,128]{2,1,0:T(8,128)S(1)} %broadcast_in_dim.25.c_ref, ...), custom_call_target="tpu_custom_call" | custom-call | flops 16777216 | bytes 2097152 | tf_op jit(solution)/shard_map/pallas_call | solution.py:199
  21.1 0.0 copy-done.6
  21.1 0.0 copy-done.7
  21.1 0.0 copy-done.8
  21.1 2.0 %fusion.4.gated_ref = bf16[128,1024]{1,0:T(8,128)(2,1)S(1)} fusion(bf16[128,1024]{1,0:T(8,128)(2,1)S(1)} %copy-done.7, bf16[128,1024]{1,0:T(8,128)(2,1)S(1)} %copy-done.3, f32[128,1024]{1,0:T(8,128)S(1)} %get-tuple-element.12, f32[128,1024]{1,0:T(8,128)S(1)} %get-tuple-element.13, f32[1024]{0:T(1024)S(1)} %copy-done.8, f32[1024]{0:T(1024)S(1)} %bitcast.71, ...), kind=kLoop, calls=%fused_computation.6 | loop fusion | flops 9699328 | bytes 1978368 | tf_op jit(solution)/shard_map/convert_element_type | solution.py:647
  23.1 0.0 copy-done.1
  23.1 0.0 copy-done.4
  23.1 0.0 copy-done.5
  23.1 63.9 %shard_map.155 = bf16[32,2048]{1,0:T(8,128)(2,1)S(1)} custom-call(bf16[128,1024]{1,0:T(8,128)(2,1)S(1)} %fusion.4.gated_ref, bf16[32,2048]{1,0:T(8,128)(2,1)S(1)} %copy-done.4, f32[1,2048]{1,0:T(1,128)S(1)} %bitcast.67, bf16[64,32]{1,0:T(8,128)(2,1)S(1)} %convert_element_type.12.select_ref, f32[32,64]{1,0:T(8,128)S(1)} %select_reduce_fusion.combine_ref, ...), custom_call_target="tpu_custom_call" | custom-call | flops 6442450944 | bytes 12582912 | tf_op jit(solution)/shard_map/pallas_call | solution.py:465
  87.0 0.7 copy.26
  (5 shorter events, 0.1 us)
Async XLA Ops:
  0.0 21.1 %copy-start.6 = (f32[16,128]{1,0:T(8,128)S(1)}, f32[16,128]{1,0:T(8,128)}, u32[]{:S(2)}) copy-start(f32[16,128]{1,0:T(8,128)} %param.20) | copy-start | bytes 24580
  0.0 21.1 %copy-start.7 = (bf16[128,1024]{1,0:T(8,128)(2,1)S(1)}, bf16[128,1024]{1,0:T(8,128)(2,1)}, u32[]{:S(2)}) copy-start(bf16[128,1024]{1,0:T(8,128)(2,1)} %param.17) | copy-start | bytes 786436
  0.0 21.1 %copy-start.8 = (f32[1024]{0:T(1024)S(1)}, f32[1024]{0:T(1024)}, u32[]{:S(2)}) copy-start(f32[1024]{0:T(1024)} %param.22) | copy-start | bytes 12292
  4.0 0.8 copy-start
  4.8 1.0 %copy-start.2 = (f32[128,1024]{1,0:T(8,128)S(1)}, f32[128,1024]{1,0:T(8,128)}, u32[]{:S(2)}) copy-start(f32[128,1024]{1,0:T(8,128)} %raw_ref.1) | copy-start | bytes 1572868
  5.9 0.9 %copy-start.3 = (bf16[128,1024]{1,0:T(8,128)(2,1)S(1)}, bf16[128,1024]{1,0:T(8,128)(2,1)}, u32[]{:S(2)}) copy-start(bf16[128,1024]{1,0:T(8,128)(2,1)} %x_ref.1) | copy-start | bytes 786436
  6.8 16.2 %copy-start.1 = (bf16[1024,2048]{1,0:T(8,128)(2,1)S(1)}, bf16[1024,2048]{1,0:T(8,128)(2,1)}, u32[]{:S(2)}) copy-start(bf16[1024,2048]{1,0:T(8,128)(2,1)} %proj_hbm.1) | copy-start | bytes 12582916
  6.8 16.3 %copy-start.4 = (bf16[32,2048]{1,0:T(8,128)(2,1)S(1)}, bf16[32,2048]{1,0:T(8,128)(2,1)}, u32[]{:S(2)}) copy-start(bf16[32,2048]{1,0:T(8,128)(2,1)} %residual_hbm.1) | copy-start | bytes 393220
  6.8 16.3 %copy-start.5 = (f32[2048]{0:T(1024)S(1)}, f32[2048]{0:T(1024)}, u32[]{:S(2)}) copy-start(f32[2048]{0:T(1024)} %param.25) | copy-start | bytes 24580
